TPU v7x, 32 devices: a whole 2x2x4 slice. The times are simulated.
32 devices in a mesh: segment: 4 (over y, x), dp: 8 (over z, core).
Axes of the slice: x: 2, y: 2, z: 4, core: 2. Of those that a mesh axis runs over, the one named last changes fastest.
Arguments:
- patches: bfloat16 [6272, 768], P('dp'), may hold values from -6 to 6
- region_mask: int32 [6272], P('dp'), may hold values 0 or 1
- conv_weight: bfloat16 [2, 9, 768], P(None, None, 'dp'), may hold values from -2 to 2
- conv_bias: bfloat16 [2, 768], P(None, 'dp'), may hold values from -1.75 to 1.75
- mixer_gain: bfloat16 [2, 768], P(None, 'dp'), may hold values from 0.099609375 to 1.8984375
- mixer_shift: bfloat16 [2, 768], P(None, 'dp'), may hold values from -1.75 to 1.75
- triple_weight: bfloat16 [2, 768, 2304], P(None, 'dp'), may hold values from -0.21875 to 0.21875
- triple_bias: bfloat16 [2, 2304], P(None, 'dp'), may hold values from -1.75 to 1.75
- output_weight: bfloat16 [2, 768, 768], P(None, 'dp'), may hold values from -0.625 to 0.625
- output_bias: bfloat16 [2, 768], P(None, 'dp'), may hold values from -1.75 to 1.75
- feed_gain: bfloat16 [2, 768], P(None, 'dp'), may hold values from 0.099609375 to 1.8984375
- feed_shift: bfloat16 [2, 768], P(None, 'dp'), may hold values from -1.75 to 1.75
- expand_weight: bfloat16 [2, 768, 3072], P(None, 'dp'), may hold values from -0.21875 to 0.21875
- expand_bias: bfloat16 [2, 3072], P(None, 'dp'), may hold values from -3 to 3
- reduce_weight: bfloat16 [2, 3072, 768], P(None, 'dp'), may hold values from -0.109375 to 0.109375
- reduce_bias: bfloat16 [2, 768], P(None, 'dp'), may hold values from -1.75 to 1.75
- cotangent: bfloat16 [6272, 768], P('dp'), may hold values from -6 to 6
Outputs:
- section_outputs: bfloat16 [4, 6272, 768], P('segment', 'dp')
- section_grads: bfloat16 [4, 6272, 768], P('segment', 'dp')
- grad_conv_weight: float32 [2, 9, 768], P(None, None, 'dp')
- grad_conv_bias: float32 [2, 768], P(None, 'dp')
- grad_mixer_gain: float32 [2, 768], P(None, 'dp')
- grad_mixer_shift: float32 [2, 768], P(None, 'dp')
- grad_triple_weight: float32 [2, 768, 2304], P(None, 'dp')
- grad_triple_bias: float32 [2, 2304], P(None, 'dp')
- grad_output_weight: float32 [2, 768, 768], P(None, 'dp')
- grad_output_bias: float32 [2, 768], P(None, 'dp')
- grad_feed_gain: float32 [2, 768], P(None, 'dp')
- grad_feed_shift: float32 [2, 768], P(None, 'dp')
- grad_expand_weight: float32 [2, 768, 3072], P(None, 'dp')
- grad_expand_bias: float32 [2, 3072], P(None, 'dp')
- grad_reduce_weight: float32 [2, 3072, 768], P(None, 'dp')
- grad_reduce_bias: float32 [2, 768], P(None, 'dp')
All inputs are finite; a program needn't handle non-finite values. No bound on the sum of `region_mask` on one device may be relied on, other than what follows from the above.
Results may differ from a plain program's by a relative error of at most 0.025.
Values may be sent and summed in bfloat16 or wider, within the bound.
A program may use at most 704 MiB of HBM per device.

v0:
```python
from functools import partial

import jax
import jax.numpy as jnp
from jax import lax
from jax.sharding import PartitionSpec as P

HD = 32
SIDE = 7
MICRO = 4
IMG_MB = 4


EPSILON = 1e-05


def as_sent(x):

    def short(part):
        return part.astype(jnp.bfloat16) if part.dtype == jnp.float32 else part

    return jax.tree.map(short, x)


def shifted_2(x, axis, by):
    count = lax.axis_size(axis)
    pairs = [(i, i + by) for i in range(count) if 0 <= i + by < count]
    return lax.ppermute(x, axis, pairs)


def dot_last(first_operand, second_operand):
    return lax.dot_general(
        first_operand, second_operand, (((1,), (1,)), ((), ())), preferred_element_type=jnp.float32
    )


def dot_first(first_operand, second_operand):
    return lax.dot_general(
        first_operand, second_operand, (((0,), (0,)), ((), ())), preferred_element_type=jnp.float32
    )


def layer_norm(values, norm_gain, norm_shift):
    center = values - jnp.mean(values, axis=-1, keepdims=True)
    spread = jnp.mean(center * center, axis=-1, keepdims=True)
    return center * lax.rsqrt(spread + EPSILON) * norm_gain + norm_shift


def position_conv(stream, conv_weight, conv_bias):
    features = stream.shape[-1]
    planes = stream.reshape(-1, SIDE, SIDE, features)
    padded = jnp.pad(planes, ((0, 0), (1, 1), (1, 1), (0, 0)))
    summed = jnp.zeros_like(planes) + conv_bias
    for tap_row in range(3):
        for tap_col in range(3):
            summed = (
                summed
                + padded[:, tap_row : tap_row + SIDE, tap_col : tap_col + SIDE, :]
                * conv_weight[tap_row * 3 + tap_col]
            )
    return stream + summed.reshape(stream.shape)


def front_part(stream, conv_weight, conv_bias, norm_gain, norm_shift):
    shifted = position_conv(stream, conv_weight, conv_bias)
    return (shifted, layer_norm(shifted, norm_gain, norm_shift))


def gelu_exact(values):
    return jax.nn.gelu(values, approximate=False)


def softmax_rows(scores):
    row_max = jnp.max(scores, axis=-1, keepdims=True)
    lifted = jnp.exp(scores - row_max)
    return lifted / jnp.sum(lifted, axis=-1, keepdims=True)


def window_forward(triple):
    tokens = triple.shape[0]
    features = triple.shape[1] // 3
    pieces = triple.reshape(tokens // (SIDE * SIDE), SIDE * SIDE, 3, features // HD, HD)
    queries = pieces[:, :, 0]
    key_parts = pieces[:, :, 1]
    value_parts = pieces[:, :, 2]
    scores = jnp.einsum(
        "iqhd,ikhd->ihqk", queries, key_parts, preferred_element_type=jnp.float32
    ) * HD ** (-0.5)
    softmaxed = softmax_rows(scores)
    softmaxed_low = softmaxed.astype(jnp.bfloat16)
    mixture = jnp.einsum(
        "ihqk,ikhd->iqhd", softmaxed_low, value_parts, preferred_element_type=jnp.float32
    )
    return (
        mixture.reshape(tokens, features),
        (queries, key_parts, value_parts, softmaxed, softmaxed_low),
    )


def window_backward(stored, grad_mixture):
    queries, key_parts, value_parts, softmaxed, softmaxed_low = stored
    grad_pieces = grad_mixture.reshape(queries.shape)
    grad_values = jnp.einsum(
        "ihqk,iqhd->ikhd", softmaxed_low, grad_pieces, preferred_element_type=jnp.float32
    )
    grad_soft = jnp.einsum(
        "iqhd,ikhd->ihqk", grad_pieces, value_parts, preferred_element_type=jnp.float32
    )
    grad_scores = (
        softmaxed * (grad_soft - jnp.sum(grad_soft * softmaxed, axis=-1, keepdims=True))
    ).astype(jnp.bfloat16)
    grad_queries = jnp.einsum(
        "ihqk,ikhd->iqhd", grad_scores, key_parts, preferred_element_type=jnp.float32
    ) * HD ** (-0.5)
    grad_keys = jnp.einsum(
        "ihqk,iqhd->ikhd", grad_scores, queries, preferred_element_type=jnp.float32
    ) * HD ** (-0.5)
    joined = jnp.stack([grad_queries, grad_keys, grad_values], axis=2)
    return joined.reshape(grad_mixture.shape[0], 3 * grad_mixture.shape[1])


def channel_forward(triple, mask_rows):
    tokens = triple.shape[0]
    features = triple.shape[1] // 3
    images = tokens // (SIDE * SIDE)
    pieces = triple.reshape(images, SIDE * SIDE, 3, features // HD, HD)
    queries = pieces[:, :, 0]
    keep_mask = mask_rows.reshape(images, SIDE * SIDE, 1, 1).astype(jnp.bfloat16)
    masked = pieces[:, :, 1] * keep_mask
    value_parts = pieces[:, :, 2]
    scores = jnp.einsum(
        "itgc,itge->igce", queries, masked, preferred_element_type=jnp.float32
    ) * HD ** (-0.5)
    softmaxed = softmax_rows(scores)
    softmaxed_low = softmaxed.astype(jnp.bfloat16)
    mixture = jnp.einsum(
        "igce,itge->itgc", softmaxed_low, value_parts, preferred_element_type=jnp.float32
    )
    return (
        mixture.reshape(tokens, features),
        (queries, masked, value_parts, keep_mask, softmaxed, softmaxed_low),
    )


def channel_backward(stored, grad_mixture):
    queries, masked, value_parts, keep_mask, softmaxed, softmaxed_low = stored
    grad_pieces = grad_mixture.reshape(queries.shape)
    grad_soft = jnp.einsum(
        "itgc,itge->igce", grad_pieces, value_parts, preferred_element_type=jnp.float32
    )
    grad_values = jnp.einsum(
        "igce,itgc->itge", softmaxed_low, grad_pieces, preferred_element_type=jnp.float32
    )
    grad_scores = (
        softmaxed * (grad_soft - jnp.sum(grad_soft * softmaxed, axis=-1, keepdims=True))
    ).astype(jnp.bfloat16)
    grad_queries = jnp.einsum(
        "igce,itge->itgc", grad_scores, masked, preferred_element_type=jnp.float32
    ) * HD ** (-0.5)
    grad_masked = jnp.einsum(
        "igce,itgc->itge", grad_scores, queries, preferred_element_type=jnp.float32
    ) * HD ** (-0.5)
    grad_keys = grad_masked * keep_mask.astype(jnp.float32)
    joined = jnp.stack([grad_queries, grad_keys, grad_values], axis=2)
    return joined.reshape(grad_mixture.shape[0], 3 * grad_mixture.shape[1])


def mixer_inner(stream, weights, mask_rows, channel):
    (
        conv_weight,
        conv_bias,
        norm_gain,
        norm_shift,
        triple_weight,
        triple_bias,
        output_weight,
        output_bias,
    ) = weights[:8]
    widened = stream.astype(jnp.float32)
    (shifted, normed), front_pull = jax.vjp(
        front_part,
        widened,
        conv_weight.astype(jnp.float32),
        conv_bias.astype(jnp.float32),
        norm_gain.astype(jnp.float32),
        norm_shift.astype(jnp.float32),
    )
    normed_low = normed.astype(jnp.bfloat16)
    triple = (
        jnp.dot(normed_low, triple_weight, preferred_element_type=jnp.float32)
        + triple_bias.astype(jnp.float32)
    ).astype(jnp.bfloat16)
    if channel:
        mixture, stored = channel_forward(triple, mask_rows)
    else:
        mixture, stored = window_forward(triple)
    mixture_low = mixture.astype(jnp.bfloat16)
    return (shifted, front_pull, normed_low, stored, mixture_low)


def mixer_forward(stream, weights, mask_rows, channel):
    shifted, front_pull, normed_low, stored, mixture_low = mixer_inner(
        stream, weights, mask_rows, channel
    )
    result = (
        shifted
        + jnp.dot(mixture_low, weights[6], preferred_element_type=jnp.float32)
        + weights[7].astype(jnp.float32)
    )
    return result.astype(jnp.bfloat16)


def mixer_backward(stream, grad_out, weights, mask_rows, channel):
    shifted, front_pull, normed_low, stored, mixture_low = mixer_inner(
        stream, weights, mask_rows, channel
    )
    grad_wide = grad_out.astype(jnp.float32)
    grad_out_bias = jnp.sum(grad_wide, axis=0)
    grad_out_weight = dot_first(mixture_low, grad_out)
    grad_mixture = dot_last(grad_out, weights[6]).astype(jnp.bfloat16)
    if channel:
        grad_triple = channel_backward(stored, grad_mixture).astype(jnp.bfloat16)
    else:
        grad_triple = window_backward(stored, grad_mixture).astype(jnp.bfloat16)
    grad_tri_weight = dot_first(normed_low, grad_triple)
    grad_tri_bias = jnp.sum(grad_triple.astype(jnp.float32), axis=0)
    grad_normed = dot_last(grad_triple, weights[4])
    grad_stream, grad_taps, grad_tap_bias, grad_gain, grad_shift = front_pull(
        (grad_wide, grad_normed)
    )
    zero_tail = tuple((jnp.zeros(member.shape, jnp.float32) for member in weights[8:]))
    return (
        grad_stream.astype(jnp.bfloat16),
        (
            grad_taps,
            grad_tap_bias,
            grad_gain,
            grad_shift,
            grad_tri_weight,
            grad_tri_bias,
            grad_out_weight,
            grad_out_bias,
        )
        + zero_tail,
    )


def feed_inner(stream, weights):
    norm_gain, norm_shift, expand_weight, expand_bias, reduce_weight, reduce_bias = weights[8:]
    widened = stream.astype(jnp.float32)
    normed, norm_pull = jax.vjp(
        layer_norm, widened, norm_gain.astype(jnp.float32), norm_shift.astype(jnp.float32)
    )
    normed_low = normed.astype(jnp.bfloat16)
    hidden = jnp.dot(
        normed_low, expand_weight, preferred_element_type=jnp.float32
    ) + expand_bias.astype(jnp.float32)
    active, gelu_pull = jax.vjp(gelu_exact, hidden)
    return (widened, norm_pull, normed_low, gelu_pull, active.astype(jnp.bfloat16))


def feed_forward(stream, weights):
    widened, norm_pull, normed_low, gelu_pull, active_low = feed_inner(stream, weights)
    result = (
        widened
        + jnp.dot(active_low, weights[12], preferred_element_type=jnp.float32)
        + weights[13].astype(jnp.float32)
    )
    return result.astype(jnp.bfloat16)


def feed_backward(stream, grad_out, weights):
    widened, norm_pull, normed_low, gelu_pull, active_low = feed_inner(stream, weights)
    grad_wide = grad_out.astype(jnp.float32)
    grad_red_bias = jnp.sum(grad_wide, axis=0)
    grad_red_weight = dot_first(active_low, grad_out)
    grad_active = dot_last(grad_out, weights[12])
    grad_hidden = gelu_pull(grad_active)[0].astype(jnp.bfloat16)
    grad_exp_weight = dot_first(normed_low, grad_hidden)
    grad_exp_bias = jnp.sum(grad_hidden.astype(jnp.float32), axis=0)
    grad_normed = dot_last(grad_hidden, weights[10])
    grad_inner, grad_gain, grad_shift = norm_pull(grad_normed)
    zero_head = tuple((jnp.zeros(member.shape, jnp.float32) for member in weights[:8]))
    grad_stream = grad_wide + grad_inner
    return (
        grad_stream.astype(jnp.bfloat16),
        zero_head
        + (grad_gain, grad_shift, grad_exp_weight, grad_exp_bias, grad_red_weight, grad_red_bias),
    )


def section_forward(section, stream, weights, mask_rows):
    if section % 2 == 1:
        return feed_forward(stream, weights)
    return mixer_forward(stream, weights, mask_rows, section == 2)


def section_backward(section, stream, grad_out, weights, mask_rows):
    if section % 2 == 1:
        return feed_backward(stream, grad_out, weights)
    return mixer_backward(stream, grad_out, weights, mask_rows, section == 2)


def spare_forward(stream, weights, mask_rows):
    return jnp.zeros_like(stream)


def spare_backward(stream, grad_out, weights, mask_rows):
    return (
        jnp.zeros_like(stream),
        tuple((jnp.zeros(member.shape, jnp.float32) for member in weights)),
    )


def put_rows(buffer, rows, row_start, is_live):
    former = lax.dynamic_slice_in_dim(buffer, row_start, rows.shape[0], 0)
    return lax.dynamic_update_slice_in_dim(buffer, jnp.where(is_live, rows, former), row_start, 0)


def run_segments(layer_set, patches, region_mask, cotangent, segment_index, segments):
    features = patches.shape[1]
    micro_count = MICRO
    micro_rows = IMG_MB * SIDE * SIDE
    tick_count = micro_count + segments - 1
    forward_branches = [
        partial(section_forward, 0),
        partial(section_forward, 1),
        partial(section_forward, 2),
        partial(section_forward, 3),
        spare_forward,
    ]
    backward_branches = [
        partial(section_backward, 0),
        partial(section_backward, 1),
        partial(section_backward, 2),
        partial(section_backward, 3),
        spare_backward,
    ]
    received = jnp.zeros((micro_rows, features), jnp.bfloat16)
    kept_inputs = jnp.zeros((micro_count * micro_rows, features), jnp.bfloat16)
    outputs_here = jnp.zeros((micro_count * micro_rows, features), jnp.bfloat16)
    for tick_index in range(tick_count):
        micro_index = tick_index - segment_index
        is_live = (micro_index >= 0) & (micro_index < micro_count)
        row_start = jnp.clip(micro_index, 0, micro_count - 1) * micro_rows
        fresh_rows = lax.dynamic_slice_in_dim(patches, row_start, micro_rows, 0)
        mask_rows = lax.dynamic_slice_in_dim(region_mask, row_start, micro_rows, 0)
        entering = jnp.where(segment_index == 0, fresh_rows, received)
        leaving = lax.switch(
            jnp.where(is_live, segment_index, segments),
            forward_branches,
            entering,
            layer_set,
            mask_rows,
        )
        kept_inputs = put_rows(kept_inputs, entering, row_start, is_live)
        outputs_here = put_rows(outputs_here, leaving, row_start, is_live)
        if tick_index + 1 < tick_count:
            received = jax.tree.map(
                lambda part, own: part.astype(own.dtype),
                shifted_2(as_sent(leaving), "segment", 1),
                leaving,
            )
    grad_received = jnp.zeros((micro_rows, features), jnp.bfloat16)
    grads_here = jnp.zeros((micro_count * micro_rows, features), jnp.bfloat16)
    totals = tuple((jnp.zeros(member.shape, jnp.float32) for member in layer_set))
    for tick_index in range(tick_count):
        micro_index = tick_index - (segments - 1 - segment_index)
        is_live = (micro_index >= 0) & (micro_index < micro_count)
        row_start = jnp.clip(micro_index, 0, micro_count - 1) * micro_rows
        seed_rows = lax.dynamic_slice_in_dim(cotangent, row_start, micro_rows, 0)
        mask_rows = lax.dynamic_slice_in_dim(region_mask, row_start, micro_rows, 0)
        arriving = jnp.where(segment_index == segments - 1, seed_rows, grad_received)
        stream = lax.dynamic_slice_in_dim(kept_inputs, row_start, micro_rows, 0)
        grad_stream, grad_terms = lax.switch(
            jnp.where(is_live, segment_index, segments),
            backward_branches,
            stream,
            arriving,
            layer_set,
            mask_rows,
        )
        totals = tuple(
            (first_term + second_term for first_term, second_term in zip(totals, grad_terms))
        )
        grads_here = put_rows(grads_here, grad_stream, row_start, is_live)
        if tick_index + 1 < tick_count:
            grad_received = jax.tree.map(
                lambda part, own: part.astype(own.dtype),
                shifted_2(as_sent(grad_stream), "segment", -1),
                grad_stream,
            )
    return (outputs_here, grads_here, totals)


def body(
    patches,
    region_mask,
    conv_weight,
    conv_bias,
    mixer_gain,
    mixer_shift,
    triple_weight,
    triple_bias,
    output_weight,
    output_bias,
    feed_gain,
    feed_shift,
    expand_weight,
    expand_bias,
    reduce_weight,
    reduce_bias,
    cotangent,
):
    params = (
        conv_weight,
        conv_bias,
        mixer_gain,
        mixer_shift,
        triple_weight,
        triple_bias,
        output_weight,
        output_bias,
        feed_gain,
        feed_shift,
        expand_weight,
        expand_bias,
        reduce_weight,
        reduce_bias,
    )
    segments = lax.axis_size("segment")
    segment_index = lax.axis_index("segment")
    layer_index = segment_index // 2
    slices = tuple(
        (lax.dynamic_index_in_dim(member, layer_index, 0, keepdims=False) for member in params)
    )
    layer_set = (
        lax.all_gather(slices[0], "dp", axis=1, tiled=True),
        lax.all_gather(slices[1], "dp", axis=0, tiled=True),
        lax.all_gather(slices[2], "dp", axis=0, tiled=True),
        lax.all_gather(slices[3], "dp", axis=0, tiled=True),
        lax.all_gather(slices[4], "dp", axis=0, tiled=True),
        lax.all_gather(slices[5], "dp", axis=0, tiled=True),
        lax.all_gather(slices[6], "dp", axis=0, tiled=True),
        lax.all_gather(slices[7], "dp", axis=0, tiled=True),
        lax.all_gather(slices[8], "dp", axis=0, tiled=True),
        lax.all_gather(slices[9], "dp", axis=0, tiled=True),
        lax.all_gather(slices[10], "dp", axis=0, tiled=True),
        lax.all_gather(slices[11], "dp", axis=0, tiled=True),
        lax.all_gather(slices[12], "dp", axis=0, tiled=True),
        lax.all_gather(slices[13], "dp", axis=0, tiled=True),
    )
    outputs_here, grads_here, totals = run_segments(
        layer_set, patches, region_mask, cotangent, segment_index, segments
    )
    reduced = (
        lax.psum_scatter(totals[0], "dp", scatter_dimension=1, tiled=True),
        lax.psum_scatter(totals[1], "dp", scatter_dimension=0, tiled=True),
        lax.psum_scatter(totals[2], "dp", scatter_dimension=0, tiled=True),
        lax.psum_scatter(totals[3], "dp", scatter_dimension=0, tiled=True),
        lax.psum_scatter(totals[4], "dp", scatter_dimension=0, tiled=True),
        lax.psum_scatter(totals[5], "dp", scatter_dimension=0, tiled=True),
        lax.psum_scatter(totals[6], "dp", scatter_dimension=0, tiled=True),
        lax.psum_scatter(totals[7], "dp", scatter_dimension=0, tiled=True),
        lax.psum_scatter(totals[8], "dp", scatter_dimension=0, tiled=True),
        lax.psum_scatter(totals[9], "dp", scatter_dimension=0, tiled=True),
        lax.psum_scatter(totals[10], "dp", scatter_dimension=0, tiled=True),
        lax.psum_scatter(totals[11], "dp", scatter_dimension=0, tiled=True),
        lax.psum_scatter(totals[12], "dp", scatter_dimension=0, tiled=True),
        lax.psum_scatter(totals[13], "dp", scatter_dimension=0, tiled=True),
    )
    placed = tuple(
        (
            jnp.stack(
                [jnp.where(layer_index == 0, member, 0.0), jnp.where(layer_index == 1, member, 0.0)]
            )
            for member in reduced
        )
    )
    section_outputs = outputs_here[None]
    section_grads = grads_here[None]
    summed = (
        lax.psum(placed[0].astype(jnp.bfloat16), "segment").astype(jnp.float32),
        lax.psum(placed[1].astype(jnp.bfloat16), "segment").astype(jnp.float32),
        lax.psum(placed[2].astype(jnp.bfloat16), "segment").astype(jnp.float32),
        lax.psum(placed[3].astype(jnp.bfloat16), "segment").astype(jnp.float32),
        lax.psum(placed[4].astype(jnp.bfloat16), "segment").astype(jnp.float32),
        lax.psum(placed[5].astype(jnp.bfloat16), "segment").astype(jnp.float32),
        lax.psum(placed[6].astype(jnp.bfloat16), "segment").astype(jnp.float32),
        lax.psum(placed[7].astype(jnp.bfloat16), "segment").astype(jnp.float32),
        lax.psum(placed[8].astype(jnp.bfloat16), "segment").astype(jnp.float32),
        lax.psum(placed[9].astype(jnp.bfloat16), "segment").astype(jnp.float32),
        lax.psum(placed[10].astype(jnp.bfloat16), "segment").astype(jnp.float32),
        lax.psum(placed[11].astype(jnp.bfloat16), "segment").astype(jnp.float32),
        lax.psum(placed[12].astype(jnp.bfloat16), "segment").astype(jnp.float32),
        lax.psum(placed[13].astype(jnp.bfloat16), "segment").astype(jnp.float32),
    )
    return (
        section_outputs,
        section_grads,
        summed[0],
        summed[1],
        summed[2],
        summed[3],
        summed[4],
        summed[5],
        summed[6],
        summed[7],
        summed[8],
        summed[9],
        summed[10],
        summed[11],
        summed[12],
        summed[13],
    )


def solution(mesh):
    in_specs = (
        P("dp", None),
        P("dp"),
        P(None, None, "dp"),
        P(None, "dp"),
        P(None, "dp"),
        P(None, "dp"),
        P(None, "dp", None),
        P(None, "dp"),
        P(None, "dp", None),
        P(None, "dp"),
        P(None, "dp"),
        P(None, "dp"),
        P(None, "dp", None),
        P(None, "dp"),
        P(None, "dp", None),
        P(None, "dp"),
        P("dp", None),
    )
    out_specs = (
        P("segment", "dp", None),
        P("segment", "dp", None),
        P(None, None, "dp"),
        P(None, "dp"),
        P(None, "dp"),
        P(None, "dp"),
        P(None, "dp", None),
        P(None, "dp"),
        P(None, "dp", None),
        P(None, "dp"),
        P(None, "dp"),
        P(None, "dp"),
        P(None, "dp", None),
        P(None, "dp"),
        P(None, "dp", None),
        P(None, "dp"),
    )
    return jax.shard_map(body, mesh=mesh, in_specs=in_specs, out_specs=out_specs, check_vma=False)
```

profile of v0, /device:TPU:16, one launch (start us, length us, event | category | flops | bytes accessed | tf_op | source)
XLA Modules:
  0.0 1719.9 jit_solution(15904271227485779164)
XLA Ops:
  15.0 14.0 all-gather.1
  31.0 12.9 all-gather.11
  44.3 23.8 %all-reduce.298 = (bf16[768]{0:T(1024)(128)(2,1)S(1)}, bf16[768]{0:T(1024)(128)(2,1)S(1)}, bf16[768]{0:T(1024)(128)(2,1)S(1)}, bf16[2304]{0:T(1024)(128)(2,1)S(1...) all-reduce(bf16[768]{0:T(1024)(128)(2,1)S(1)} %dynamic-update-slice, ...), channel_id=2, replica_groups=mesh['segment'=4,'dp'=8] {'dp'}, use_global_device_ids=true, to_apply=%add.280 | all-reduce | flops 7680 | bytes 30720 | tf_op jit(solution)/shard_map/all_gather | solution.py:439
  69.2 9.7 all-gather.19.cloned.1.call-done
  79.0 52.8 %all-gather.23.cloned.1.call-done = bf16[1,768,3072]{2,1,0:T(8,128)(2,1)} async-done(((bf16[1,96,3072]{2,1,0:T(8,128)(2,1)}), bf16[1,768,3072]{2,1,0:T(8,128)(2,1)}) %all-gather.23.cloned.1.call-update) | async-done | bytes 4718608 | tf_op jit(solution)/shard_map/all_gather | solution.py:448
  131.7 52.6 %all-gather.25.cloned.1.call-done = bf16[1,3072,768]{2,1,0:T(8,128)(2,1)} async-done(((bf16[1,384,768]{2,1,0:T(8,128)(2,1)}), bf16[1,3072,768]{2,1,0:T(8,128)(2,1)}) %all-gather.25.cloned.1.call-update) | async-done | bytes 4718608 | tf_op jit(solution)/shard_map/all_gather | solution.py:450
  184.4 46.2 %conditional.14 = (bf16[196,768]{1,0:T(8,128)(2,1)}) conditional(s32[]{:T(128)} %clamp.42, (bf16[196,768]{1,0:T(8,128)(2,1)S(1)}, bf16[768]{0:T(1024)(128)(2,1)S(1)}, bf16[9,768]{1,0:T(8,128)(2,1)S(1)}, bf16[768]{0:T(1024)(128)(2,1)S(1)}, bf16[768]{0:T(1024)(128)(2,1)S(1)}, /*index=5*/bf16[768,2304]{1,0:T(8,128)(2,1)}, ...), branch_computations={%region_0.5_spmd, %region_5.8_spmd, %region_8.13_spmd, %region_13.... | conditional | flops 1891841536 | bytes 29605044 | solution.py:349
  241.5 56.5 %conditional.15 = (bf16[196,768]{1,0:T(8,128)(2,1)}) conditional(s32[]{:T(128)} %clamp.43, (bf16[196,768]{1,0:T(8,128)(2,1)S(1)}, bf16[768]{0:T(1024)(128)(2,1)S(1)}, bf16[9,768]{1,0:T(8,128)(2,1)S(1)}, bf16[768]{0:T(1024)(128)(2,1)S(1)}, bf16[768]{0:T(1024)(128)(2,1)S(1)}, /*index=5*/bf16[768,2304]{1,0:T(8,128)(2,1)}, ...), branch_computations={%region_17.22_spmd, %region_22.25_spmd, %region_25.30_spmd, %regio... | conditional | flops 1891841536 | bytes 24886424 | solution.py:349
  308.2 56.6 %conditional.16 = (bf16[196,768]{1,0:T(8,128)(2,1)}) conditional(s32[]{:T(128)} %clamp.44, (bf16[196,768]{1,0:T(8,128)(2,1)S(1)}, bf16[768]{0:T(1024)(128)(2,1)S(1)}, bf16[9,768]{1,0:T(8,128)(2,1)S(1)}, bf16[768]{0:T(1024)(128)(2,1)S(1)}, bf16[768]{0:T(1024)(128)(2,1)S(1)}, /*index=5*/bf16[768,2304]{1,0:T(8,128)(2,1)}, ...), branch_computations={%region_34.39_spmd, %region_39.42_spmd, %region_42.47_spmd, %regio... | conditional | flops 1891841536 | bytes 24886424 | solution.py:349
  374.5 56.6 %conditional.17 = (bf16[196,768]{1,0:T(8,128)(2,1)}) conditional(s32[]{:T(128)} %clamp.45, (bf16[196,768]{1,0:T(8,128)(2,1)S(1)}, bf16[768]{0:T(1024)(128)(2,1)S(1)}, bf16[9,768]{1,0:T(8,128)(2,1)S(1)}, bf16[768]{0:T(1024)(128)(2,1)S(1)}, bf16[768]{0:T(1024)(128)(2,1)S(1)}, /*index=5*/bf16[768,2304]{1,0:T(8,128)(2,1)}, ...), branch_computations={%region_51.56_spmd, %region_56.59_spmd, %region_59.64_spmd, %regio... | conditional | flops 1891841536 | bytes 24886424 | solution.py:349
  440.0 17.9 %conditional.18 = (bf16[196,768]{1,0:T(8,128)(2,1)}) conditional(s32[]{:T(128)} %clamp.46, (bf16[196,768]{1,0:T(8,128)(2,1)S(1)}, bf16[768]{0:T(1024)(128)(2,1)S(1)}, bf16[9,768]{1,0:T(8,128)(2,1)S(1)}, bf16[768]{0:T(1024)(128)(2,1)S(1)}, bf16[768]{0:T(1024)(128)(2,1)S(1)}, /*index=5*/bf16[768,2304]{1,0:T(8,128)(2,1)}, ...), branch_computations={%region_68.73_spmd, %region_73.76_spmd, %region_76.81_spmd, %regio... | conditional | flops 1891841536 | bytes 24886424 | solution.py:349
  457.9 11.0 collective-permute-start.4
  475.6 15.0 conditional.19
  504.6 33.1 %conditional.21 = (bf16[196,768]{1,0:T(8,128)(2,1)S(1)}, f32[9,768]{1,0:T(8,128)S(1)}, f32[768]{0:T(1024)S(1)}, f32[768]{0:T(1024)S(1)}, f32[768]{0:T(1024)S(1)}...) conditional(s32[]{:T(128)} %clamp.49, ...), branch_computations={%region_119.141_spmd, %region_141.150_spmd, %region_150.172_spmd, ... | conditional | flops 4715591680 | bytes 120210264 | solution.py:375
  545.0 34.1 %collective-permute-done.6 = bf16[196,768]{1,0:T(8,128)(2,1)S(1)} collective-permute-done((bf16[196,768]{1,0:T(8,128)(2,1)S(1)}, bf16[196,768]{1,0:T(8,128)(2,1)S(1)}, u32[]{:S(2)}, u32[]{:S(2)}) %collective-permute-start.6) | collective-permute-done | bytes 301088 | tf_op jit(solution)/shard_map/ppermute | solution.py:28
  580.2 42.0 %conditional.22 = (bf16[196,768]{1,0:T(8,128)(2,1)}, f32[9,768]{1,0:T(8,128)S(1)}, f32[768]{0:T(1024)}, f32[768]{0:T(1024)}, f32[768]{0:T(1024)}, /*index=5*/f32...) conditional(s32[]{:T(128)} %clamp.50, ...), branch_computations={%region_182.204_spmd, %region_204.213_spmd, %region_213.235_spmd, ... | conditional | flops 4715591680 | bytes 120781640 | solution.py:375
  624.2 8.9 collective-permute-done.7
  634.2 42.4 %conditional.23 = (bf16[196,768]{1,0:T(8,128)(2,1)}, f32[9,768]{1,0:T(8,128)S(1)}, f32[768]{0:T(1024)}, f32[768]{0:T(1024)}, f32[768]{0:T(1024)}, /*index=5*/f32...) conditional(s32[]{:T(128)} %clamp.51, ...), branch_computations={%region_245.267_spmd, %region_267.276_spmd, %region_276.298_spmd, ... | conditional | flops 4715591680 | bytes 120781640 | solution.py:375
  678.6 95.2 %collective-permute-done.8 = bf16[196,768]{1,0:T(8,128)(2,1)S(1)} collective-permute-done((bf16[196,768]{1,0:T(8,128)(2,1)}, bf16[196,768]{1,0:T(8,128)(2,1)S(1)}, u32[]{:S(2)}, u32[]{:S(2)}) %collective-permute-start.8) | collective-permute-done | bytes 301088 | tf_op jit(solution)/shard_map/ppermute | solution.py:28
  774.9 112.6 %conditional.24 = (bf16[196,768]{1,0:T(8,128)(2,1)}, f32[9,768]{1,0:T(8,128)S(1)}, f32[768]{0:T(1024)}, f32[768]{0:T(1024)}, f32[768]{0:T(1024)}, /*index=5*/f32...) conditional(s32[]{:T(128)} %clamp.52, ...), branch_computations={%region_308.330_spmd, %region_330.339_spmd, %region_339.361_spmd, ... | conditional | flops 4715591680 | bytes 120781640 | solution.py:375
  898.2 112.6 %conditional.25 = (bf16[196,768]{1,0:T(8,128)(2,1)}, f32[9,768]{1,0:T(8,128)S(1)}, f32[768]{0:T(1024)}, f32[768]{0:T(1024)}, f32[768]{0:T(1024)}, /*index=5*/f32...) conditional(s32[]{:T(128)} %clamp.53, ...), branch_computations={%region_371.393_spmd, %region_393.402_spmd, %region_402.424_spmd, ... | conditional | flops 4715591680 | bytes 120781640 | solution.py:375
  1021.6 113.7 %conditional.26 = (bf16[196,768]{1,0:T(8,128)(2,1)}, f32[9,768]{1,0:T(8,128)S(1)}, f32[768]{0:T(1024)}, f32[768]{0:T(1024)}, f32[768]{0:T(1024)}, /*index=5*/f32...) conditional(s32[]{:T(128)} %clamp.54, ...), branch_computations={%region_434.456_spmd, %region_456.465_spmd, %region_465.487_spmd, ... | conditional | flops 4715591680 | bytes 120781640 | solution.py:375
  1145.4 109.2 %conditional.27 = (bf16[196,768]{1,0:T(8,128)(2,1)S(1)}, f32[9,768]{1,0:T(8,128)S(1)}, f32[768]{0:T(1024)}, f32[768]{0:T(1024)}, f32[768]{0:T(1024)}, /*index=5*...) conditional(s32[]{:T(128)} %clamp.55, ...), branch_computations={%region_497.519_spmd, %region_519.528_spmd, %region_528.550_spmd, ... | conditional | flops 4715591680 | bytes 119077432 | solution.py:375
  1263.0 20.3 %add_add_fusion.30 = f32[768,2304]{1,0:T(8,128)} fusion(f32[768,2304]{1,0:T(8,128)} %get-tuple-element.1646, f32[768,2304]{1,0:T(8,128)} %get-tuple-element.1645, f32[768,2304]{1,0:T(8,128)} %get-tuple-element.1644, f32[768,2304]{1,0:T(8,128)} %get-tuple-element.1643, f32[768,2304]{1,0:T(8,128)} %get-tuple-element.1642, ...), kind=kLoop, calls=%fused_computation.3740 | loop fusion | flops 10616832 | bytes 56623104 | tf_op jit(solution)/shard_map/add | solution.py:384
  1283.4 27.5 %add_add_fusion.29 = f32[768,3072]{1,0:T(8,128)} fusion(f32[768,3072]{1,0:T(8,128)} %get-tuple-element.1688, f32[768,3072]{1,0:T(8,128)} %get-tuple-element.1687, f32[768,3072]{1,0:T(8,128)} %get-tuple-element.1686, f32[768,3072]{1,0:T(8,128)} %get-tuple-element.1685, f32[768,3072]{1,0:T(8,128)} %get-tuple-element.1684, ...), kind=kLoop, calls=%fused_computation.3739 | loop fusion | flops 14155776 | bytes 75497472 | tf_op jit(solution)/shard_map/add | solution.py:384
  1311.0 26.0 %add_add_fusion.28 = f32[3072,768]{1,0:T(8,128)} fusion(f32[3072,768]{1,0:T(8,128)} %get-tuple-element.1702, f32[3072,768]{1,0:T(8,128)} %get-tuple-element.1701, f32[3072,768]{1,0:T(8,128)} %get-tuple-element.1700, f32[3072,768]{1,0:T(8,128)} %get-tuple-element.1699, f32[3072,768]{1,0:T(8,128)} %get-tuple-element.1698, ...), kind=kLoop, calls=%fused_computation.3738 | loop fusion | flops 14155776 | bytes 75497472 | tf_op jit(solution)/shard_map/add | solution.py:384
  1352.4 16.4 conditional.20
  1391.1 82.7 %reduce-scatter.12.cloned.1.call-done = f32[96,3072]{1,0:T(8,128)} async-done(((f32[768,3072]{1,0:T(8,128)}), f32[96,3072]{1,0:T(8,128)}) %reduce-scatter.12.cloned.1.call-update) | async-done | bytes 1179664 | tf_op jit(solution)/shard_map/reduce_scatter | solution.py:467
  1476.4 97.6 %reduce-scatter.14.cloned.1.call-done = f32[384,768]{1,0:T(8,128)} async-done(((f32[3072,768]{1,0:T(8,128)}), f32[384,768]{1,0:T(8,128)}) %reduce-scatter.14.cloned.1.call-update) | async-done | bytes 1179664 | tf_op jit(solution)/shard_map/reduce_scatter | solution.py:469
  1577.7 23.2 %all-reduce.297 = (bf16[768]{0:T(1024)(128)(2,1)S(1)}, bf16[768]{0:T(1024)(128)(2,1)S(1)}, bf16[768]{0:T(1024)(128)(2,1)S(1)}, bf16[2304]{0:T(1024)(128)(2,1)S(1...) all-reduce(f32[768]{0:T(1024)S(1)} %add_add_fusion.41, ...), channel_id=17, replica_groups=mesh['segment'=4,'dp'=8] {'dp'}, use_global_device_ids=true, to_apply=%region_562.563.clone | all-reduce | flops 10752 | bytes 64512
  1604.4 16.2 all-reduce.299
  1626.3 79.7 %all-reduce.303.cloned.1.call-done = (bf16[2,96,2304]{2,1,0:T(8,128)(2,1)}, bf16[2,96,768]{2,1,0:T(8,128)(2,1)}, bf16[2,96,3072]{2,1,0:T(8,128)(2,1)}, bf16[2,384,768]{2,1,0:T(8,128)(2,1)}) async-done(((bf16[2,96,2304]{2,1,0:T(8,128)(2,1)}, bf16[2,96,768]{2,1,0:T(8,128)(2,1)}, bf16[2,96,3072]{2,1,0:T(8,128)(2,1)}, bf16[2,384,768]{2,1,0:T(8,128)(2,1)}), (bf16[2,96,2304]{2,1,0:T(8,128)(2,1)}, ...) | async-done | bytes 3538960 | tf_op jit(solution)/shard_map/psum | solution.py:487
  (1221 shorter events, 731.3 us)
Async XLA Ops:
  7.2 62.0 %all-gather.21.cloned.1.call-start = ((), (), s32[]{:S(2)}) async-start(), calls=%async_computation.10 | async-start | bytes 1327104 | tf_op jit(solution)/shard_map/all_gather | solution.py:444
  9.1 69.9 %all-gather.19.cloned.1.call-start = ((), (), s32[]{:S(2)}) async-start(), calls=%async_computation.9 | async-start | bytes 3981312 | tf_op jit(solution)/shard_map/all_gather | solution.py:442
  11.0 120.7 %all-gather.23.cloned.1.call-start = ((), (), s32[]{:S(2)}) async-start(), calls=%async_computation.11 | async-start | bytes 5308416 | tf_op jit(solution)/shard_map/all_gather | solution.py:448
  11.9 172.4 %copy-start.244 = (s32[784]{0:T(1024)S(1)}, s32[784]{0:T(1024)}, u32[]{:S(2)}) copy-start(s32[784]{0:T(1024)} %param.88) | copy-start | bytes 9412
  12.0 172.4 %all-gather.25.cloned.1.call-start = ((), (), s32[]{:S(2)}) async-start(), calls=%async_computation.12 | async-start | bytes 5308416 | tf_op jit(solution)/shard_map/all_gather | solution.py:450
  12.9 1374.2 %reduce-scatter.10.cloned.1.call-start = ((), (), s32[]{:S(2)}) async-start(), calls=%async_computation.6 | async-start | bytes 2654208 | tf_op jit(solution)/shard_map/reduce_scatter | solution.py:463
  68.1 407.6 %copy-start.156 = (bf16[768]{0:T(1024)(128)(2,1)}, bf16[768]{0:T(1024)(128)(2,1)S(1)}, u32[]{:S(2)}) copy-start(bf16[768]{0:T(1024)(128)(2,1)S(1)} %get-tuple-element.2541) | copy-start | bytes 4612
  68.1 407.6 %copy-start.158 = (bf16[768]{0:T(1024)(128)(2,1)}, bf16[768]{0:T(1024)(128)(2,1)S(1)}, u32[]{:S(2)}) copy-start(bf16[768]{0:T(1024)(128)(2,1)S(1)} %get-tuple-element.2544) | copy-start | bytes 4612
  68.1 512.1 %copy-start.94 = (bf16[768]{0:T(1024)(128)(2,1)}, bf16[768]{0:T(1024)(128)(2,1)S(1)}, u32[]{:S(2)}) copy-start(bf16[768]{0:T(1024)(128)(2,1)S(1)} %get-tuple-element.2542) | copy-start | bytes 4612
  68.1 512.1 %copy-start.96 = (bf16[768]{0:T(1024)(128)(2,1)}, bf16[768]{0:T(1024)(128)(2,1)S(1)}, u32[]{:S(2)}) copy-start(bf16[768]{0:T(1024)(128)(2,1)S(1)} %get-tuple-element.2543) | copy-start | bytes 4612
  230.6 8.9 collective-permute-start
  298.0 8.3 collective-permute-start.1
  364.8 7.8 collective-permute-start.2
  431.0 7.1 collective-permute-start.3
  457.9 15.8 collective-permute-start.4
  490.6 9.0 collective-permute-start.5
  543.7 35.4 %collective-permute-start.6 = (bf16[196,768]{1,0:T(8,128)(2,1)S(1)}, bf16[196,768]{1,0:T(8,128)(2,1)S(1)}, u32[]{:S(2)}, u32[]{:S(2)}) collective-permute-start(bf16[196,768]{1,0:T(8,128)(2,1)S(1)} %get-tuple-element.1605), channel_id=1, source_target_pairs={{8,0},{16,8},{24,16},{9,1},{17,9},{25,17},{10,2},{18,10},{26,18},{... | collective-permute-start | bytes 903176 | tf_op jit(solution)/shard_map/ppermute | solution.py:28
  622.8 10.2 collective-permute-start.7
  634.2 140.7 %copy-start.8 = (bf16[196,768]{1,0:T(8,128)(2,1)S(1)}, bf16[196,768]{1,0:T(8,128)(2,1)}, u32[]{:S(2)}) copy-start(bf16[196,768]{1,0:T(8,128)(2,1)} %get-tuple-element.3052) | copy-start | bytes 903172
  677.3 96.5 %collective-permute-start.8 = (bf16[196,768]{1,0:T(8,128)(2,1)}, bf16[196,768]{1,0:T(8,128)(2,1)S(1)}, u32[]{:S(2)}, u32[]{:S(2)}) collective-permute-start(bf16[196,768]{1,0:T(8,128)(2,1)} %get-tuple-element.1607), channel_id=1, source_target_pairs={{8,0},{16,8},{24,16},{9,1},{17,9},{25,17},{10,2},{18,10},{26,18},{... | collective-permute-start | bytes 903176 | tf_op jit(solution)/shard_map/ppermute | solution.py:28
  774.8 123.3 %copy-start.7 = (bf16[196,768]{1,0:T(8,128)(2,1)S(1)}, bf16[196,768]{1,0:T(8,128)(2,1)}, u32[]{:S(2)}) copy-start(bf16[196,768]{1,0:T(8,128)(2,1)} %get-tuple-element.3051) | copy-start | bytes 903172
  888.1 9.0 collective-permute-start.9
  898.2 123.3 %copy-start.6 = (bf16[196,768]{1,0:T(8,128)(2,1)S(1)}, bf16[196,768]{1,0:T(8,128)(2,1)}, u32[]{:S(2)}) copy-start(bf16[196,768]{1,0:T(8,128)(2,1)} %get-tuple-element.3050) | copy-start | bytes 903172
  1011.5 9.0 collective-permute-start.10
  1021.5 123.8 %copy-start.5 = (bf16[196,768]{1,0:T(8,128)(2,1)S(1)}, bf16[196,768]{1,0:T(8,128)(2,1)}, u32[]{:S(2)}) copy-start(bf16[196,768]{1,0:T(8,128)(2,1)} %get-tuple-element.3049) | copy-start | bytes 903172
  1135.3 9.0 collective-permute-start.11
  1263.0 125.9 %reduce-scatter.8.cloned.1.call-start = ((), (), s32[]{:S(2)}) async-start(), calls=%async_computation.5 | async-start | bytes 7962624 | tf_op jit(solution)/shard_map/reduce_scatter | solution.py:461
  1283.4 190.5 %reduce-scatter.12.cloned.1.call-start = ((), (), s32[]{:S(2)}) async-start(), calls=%async_computation.7 | async-start | bytes 10616832 | tf_op jit(solution)/shard_map/reduce_scatter | solution.py:467
  1310.9 263.1 %reduce-scatter.14.cloned.1.call-start = ((), (), s32[]{:S(2)}) async-start(), calls=%async_computation.8 | async-start | bytes 10616832 | tf_op jit(solution)/shard_map/reduce_scatter | solution.py:469
  1337.0 266.5 %reduce-scatter.16.cloned.1.call-start = ((), (), s32[]{:S(2)}) async-start(), calls=%async_computation.13 | async-start | bytes 442368
  1386.7 319.3 %all-reduce.303.cloned.1.call-start = ((), (), s32[]{:S(2)}) async-start(), calls=%async_computation.14 | async-start | bytes 7077888 | tf_op jit(solution)/shard_map/psum | solution.py:487
  1602.8 108.3 %copy-start.32 = (bf16[1,784,768]{2,1,0:T(8,128)(2,1)}, bf16[1,784,768]{2,1,0:T(8,128)(2,1)S(1)}, u32[]{:S(2)}) copy-start(bf16[1,784,768]{2,1,0:T(8,128)(2,1)S(1)} %dynamic_update_slice.85) | copy-start | bytes 3612676
  (301 other events, 1949.6 us)
Sparse Core Ops, SparseCore 0:
  10.3 24.2 all-gather.20
  36.8 42.1 all-gather.18
  81.2 50.5 all-gather.22
  133.8 50.5 all-gather.24
  1263.1 28.4 reduce-scatter.9
  1293.8 79.8 reduce-scatter.7
  1376.0 97.8 reduce-scatter.11
  1476.2 97.8 reduce-scatter.13
  1576.9 25.5 reduce-scatter.15
  1607.4 98.6 all-reduce.302
where the time goes:
time: 1730 us; the launch traced here: 1720 us
  waiting for transfers between devices  556 us (32%)
  local copies, waits for them, and re-layouts  388 us (22%)
  loops' own time  280 us (16%)
  other arithmetic  212 us (12%)
  matrix products  145 us (8%)
  blocking collectives  90.1 us (5%)
  starting transfers between devices  28.8 us (2%)
  between operations  20.6 us (1%)
    ppermute x12, waiting for transfers between devices, shifted_2(): return lax.ppermute(x, axis, pairs)  181 us
    another operation x7, loops' own time, run_segments(): lax.switch(jnp.where(is_live, segment_index, segments), backward_branches...  162 us
    another operation x7, loops' own time, run_segments(): lax.switch(jnp.where(is_live, segment_index, segments), forward_branches,...  118 us
    reduce_scatter x1, waiting for transfers between devices, body(): lax.psum_scatter(totals[12], 'dp', scatter_dimension=0, tiled=True)  97.6 us
    another operation x75, local copies, waits for them, and re-layouts  87.8 us
    reduce_scatter x1, waiting for transfers between devices, body(): lax.psum_scatter(totals[10], 'dp', scatter_dimension=0, tiled=True)  82.7 us
    add x14, other arithmetic, run_segments(): first_term + second_term  82.2 us
    psum x1, waiting for transfers between devices, body(): lax.psum(placed[4].astype(jnp.bfloat16), 'segment').astype(jnp.float32)  79.7 us
  transfers between devices with their start and end apart: 22, of which 18 were waited for; matrix products, arithmetic and copies ran while one was open for 9% of the time, Pallas kernels for 0%

commit v1 on v0

--- a/solution.py
+++ b/solution.py
@@ -3,6 +3,8 @@
 import jax
 import jax.numpy as jnp
 from jax import lax
+from jax.experimental import pallas as pl
+from jax.experimental.pallas import tpu as pltpu
 from jax.sharding import PartitionSpec as P
 
 HD = 32
@@ -515,6 +517,624 @@
     )
 
 
+W = 768
+IMG = 56
+LIVE = 49
+ROWS = 224
+PAIR = 2 * IMG
+LANES = 128
+SCALE = HD ** (-0.5)
+F32 = jnp.float32
+BF16 = jnp.bfloat16
+TAPS = [(a, b) for a in range(3) for b in range(3)]
+
+
+def mm(a, b):
+    return lax.dot_general(a, b, (((1,), (0,)), ((), ())), preferred_element_type=F32)
+
+
+def mm_nt(a, b):
+    return lax.dot_general(a, b, (((1,), (1,)), ((), ())), preferred_element_type=F32)
+
+
+def mm_tn(a, b):
+    return lax.dot_general(a, b, (((0,), (0,)), ((), ())), preferred_element_type=F32)
+
+
+def row_index(rows):
+    return lax.broadcasted_iota(jnp.int32, (rows, 1), 0)
+
+
+def live_rows(rows):
+    return lax.rem(row_index(rows), IMG) < LIVE
+
+
+def column_masks(rows):
+    place = lax.rem(row_index(rows), IMG)
+    column = lax.rem(place, SIDE)
+    live = place < LIVE
+    return [(live & (column + b - 1 >= 0) & (column + b - 1 < SIDE)).astype(F32) for b in range(3)]
+
+
+def rolled(values, by):
+    by = by % values.shape[0]
+    return values if by == 0 else pltpu.roll(values, by, 0)
+
+
+def norm_parts(values):
+    center = values - jnp.mean(values, axis=-1, keepdims=True)
+    spread = jnp.mean(center * center, axis=-1, keepdims=True)
+    rstd = lax.rsqrt(spread + EPSILON)
+    return center * rstd, rstd
+
+
+def column_sum(values):
+    return jnp.sum(values, axis=0, keepdims=True)
+
+
+def head_lanes(head):
+    lane = lax.broadcasted_iota(jnp.int32, (1, LANES), 1)
+    return (lane // HD) == head
+
+
+def only(values, mask):
+    return jnp.where(mask, values, jnp.zeros_like(values))
+
+
+def mix_forward(layer, channel, u_in, u_out, w, small, mask, bias, c_ref, xhat, rstd, n_ref, t_ref, p_ref, m_ref):
+    base = 12 * layer
+    row = lambda r: small[layer, r:r + 1, :]
+    v = u_in[...].astype(F32)
+    masks = column_masks(ROWS)
+    total = v + row(9)
+    for b in range(3):
+        part = jnp.zeros_like(v)
+        for a in range(3):
+            part = part + row(3 * a + b) * rolled(v, -(SIDE * (a - 1) + b - 1))
+        total = total + part * masks[b]
+    c = jnp.where(live_rows(ROWS), total, 0.0)
+    c_ref[...] = c
+    x, r = norm_parts(c)
+    xhat[...] = x
+    rstd[...] = r
+    n_ref[...] = (x * row(10) + row(11)).astype(BF16)
+
+    @pl.loop(0, 3)
+    def _(j):
+        cols = pl.ds(pl.multiple_of(W * j, W), W)
+        t_ref[:, cols] = (mm(n_ref[...], w[base + j]) + small[layer, pl.ds(12 + j, 1), :]).astype(BF16)
+
+    @pl.loop(0, 6)
+    def _(g):
+        qs = pl.ds(pl.multiple_of(LANES * g, LANES), LANES)
+        ks = pl.ds(pl.multiple_of(W + LANES * g, LANES), LANES)
+        vs = pl.ds(pl.multiple_of(2 * W + LANES * g, LANES), LANES)
+        for pair in range(2):
+            rows = slice(PAIR * pair, PAIR * pair + PAIR)
+            q, k, val = t_ref[rows, qs], t_ref[rows, ks], t_ref[rows, vs]
+            mix = jnp.zeros((PAIR, LANES), F32)
+            if channel:
+                for im in range(2):
+                    here = (row_index(PAIR) // IMG) == im
+                    km = k * only(mask[rows, :], here)
+                    s = mm_tn(q, km) * SCALE + bias[...]
+                    e = jnp.exp(s - jnp.max(s, axis=-1, keepdims=True))
+                    p = e / jnp.sum(e, axis=-1, keepdims=True)
+                    p_ref[g, 2 * pair + im] = p
+                    mix = mix + mm_nt(only(val, here), p.astype(BF16))
+            else:
+                for head in range(4):
+                    lanes = head_lanes(head)
+                    s = mm_nt(only(q, lanes), k) * SCALE + bias[...]
+                    e = jnp.exp(s - jnp.max(s, axis=-1, keepdims=True))
+                    p = e / jnp.sum(e, axis=-1, keepdims=True)
+                    p_ref[g, 4 * pair + head] = p
+                    mix = mix + mm(p.astype(BF16), only(val, lanes))
+            m_ref[rows, qs] = mix.astype(BF16)
+
+    out = c_ref[...] + mm(m_ref[...], w[base + 3]) + row(15)
+    u_out[...] = jnp.where(live_rows(ROWS), out, 0.0).astype(BF16)
+
+
+def mix_backward(layer, channel, u_in, g_in, g_out, w, small, mask, sg, dw, c_ref, xhat, rstd, n_ref, t_ref, p_ref, m_ref, dm_ref, dt_ref, acc):
+    base = 12 * layer
+    row = lambda r: small[layer, r:r + 1, :]
+    g = g_in[...]
+    sg[layer, 15:16, :] = column_sum(g.astype(F32))
+    dm_ref[...] = mm_nt(g, w[base + 3]).astype(BF16)
+    dw(layer, 3, m_ref, lambda: g_in[...])
+
+    @pl.loop(0, 6)
+    def _(grp):
+        qs = pl.ds(pl.multiple_of(LANES * grp, LANES), LANES)
+        ks = pl.ds(pl.multiple_of(W + LANES * grp, LANES), LANES)
+        vs = pl.ds(pl.multiple_of(2 * W + LANES * grp, LANES), LANES)
+        for pair in range(2):
+            rows = slice(PAIR * pair, PAIR * pair + PAIR)
+            q, k, val, dm = t_ref[rows, qs], t_ref[rows, ks], t_ref[rows, vs], dm_ref[rows, qs]
+            dq = jnp.zeros((PAIR, LANES), F32)
+            dk = jnp.zeros((PAIR, LANES), F32)
+            dv = jnp.zeros((PAIR, LANES), F32)
+            if channel:
+                for im in range(2):
+                    here = (row_index(PAIR) // IMG) == im
+                    keep = only(mask[rows, :], here)
+                    km = k * keep
+                    p = p_ref[grp, 2 * pair + im]
+                    dmh = only(dm, here)
+                    dp = mm_tn(dmh, val)
+                    dv = dv + mm(dmh, p.astype(BF16))
+                    ds = (p * (dp - jnp.sum(dp * p, axis=-1, keepdims=True))).astype(BF16)
+                    dq = dq + mm_nt(km, ds)
+                    dk = dk + mm(only(q, here), ds) * keep.astype(F32)
+            else:
+                for head in range(4):
+                    lanes = head_lanes(head)
+                    p = p_ref[grp, 4 * pair + head]
+                    dmh = only(dm, lanes)
+                    dp = mm_nt(dmh, val)
+                    dv = dv + mm_tn(p.astype(BF16), dmh)
+                    ds = (p * (dp - jnp.sum(dp * p, axis=-1, keepdims=True))).astype(BF16)
+                    dq = dq + mm(ds, only(k, lanes))
+                    dk = dk + mm_tn(ds, only(q, lanes))
+            dt_ref[rows, qs] = (dq * SCALE).astype(BF16)
+            dt_ref[rows, ks] = (dk * SCALE).astype(BF16)
+            dt_ref[rows, vs] = dv.astype(BF16)
+
+    acc[...] = jnp.zeros_like(acc)
+
+    @pl.loop(0, 3)
+    def _(j):
+        cols = pl.ds(pl.multiple_of(W * j, W), W)
+        acc[...] += mm_nt(dt_ref[:, cols], w[base + j])
+        sg[layer, pl.ds(12 + j, 1), :] = column_sum(dt_ref[:, cols].astype(F32))
+        dw(layer, j, n_ref, lambda: dt_ref[:, cols])
+
+    dn = acc[...]
+    x = xhat[...]
+    sg[layer, 10:11, :] = column_sum(dn * x)
+    sg[layer, 11:12, :] = column_sum(dn)
+    e = dn * row(10)
+    inner = rstd[...] * (e - jnp.mean(e, axis=-1, keepdims=True) - x * jnp.mean(e * x, axis=-1, keepdims=True))
+    dc = jnp.where(live_rows(ROWS), g_in[...].astype(F32) + inner, 0.0)
+    sg[layer, 9:10, :] = column_sum(dc)
+    v = u_in[...].astype(F32)
+    masks = column_masks(ROWS)
+    du = dc
+    for b in range(3):
+        dcm = dc * masks[b]
+        for a in range(3):
+            moved = rolled(dcm, SIDE * (a - 1) + b - 1)
+            tap = 3 * a + b
+            du = du + row(tap) * moved
+            sg[layer, tap:tap + 1, :] = column_sum(moved * v)
+    g_out[...] = jnp.where(live_rows(ROWS), du, 0.0).astype(BF16)
+
+
+ROOT_HALF = 0.5 ** 0.5
+ROOT_TWO_PI = 0.3989422804014327
+
+
+def ff_forward(layer, u_in, u_out, w, small, xhat, rstd, n_ref, slope, acc):
+    base = 12 * layer
+    row = lambda r: small[layer, r:r + 1, :]
+    x, r = norm_parts(u_in[...].astype(F32))
+    xhat[...] = x
+    rstd[...] = r
+    n_ref[...] = (x * row(16) + row(17)).astype(BF16)
+    acc[...] = u_in[...].astype(F32) + row(22)
+
+    @pl.loop(0, 4)
+    def _(j):
+        cols = pl.ds(pl.multiple_of(W * j, W), W)
+        h = mm(n_ref[...], w[base + 4 + j]) + small[layer, pl.ds(18 + j, 1), :]
+        cdf = 0.5 + 0.5 * lax.erf(h * ROOT_HALF)
+        slope[:, cols] = cdf + h * (ROOT_TWO_PI * jnp.exp(-0.5 * h * h))
+        acc[...] += mm((h * cdf).astype(BF16), w[base + 8 + j])
+
+    u_out[...] = jnp.where(live_rows(ROWS), acc[...], 0.0).astype(BF16)
+
+
+def ff_backward(layer, g_in, g_out, w, small, sg, xhat, rstd, slope, acc):
+    base = 12 * layer
+    row = lambda r: small[layer, r:r + 1, :]
+    sg[layer, 22:23, :] = column_sum(g_in[...].astype(F32))
+    acc[...] = jnp.zeros_like(acc)
+
+    @pl.loop(0, 4)
+    def _(j):
+        cols = pl.ds(pl.multiple_of(W * j, W), W)
+        dh = (mm_nt(g_in[...], w[base + 8 + j]) * slope[:, cols]).astype(BF16)
+        sg[layer, pl.ds(18 + j, 1), :] = column_sum(dh.astype(F32))
+        acc[...] += mm_nt(dh, w[base + 4 + j])
+
+    dn = acc[...]
+    x = xhat[...]
+    sg[layer, 16:17, :] = column_sum(dn * x)
+    sg[layer, 17:18, :] = column_sum(dn)
+    e = dn * row(16)
+    inner = rstd[...] * (e - jnp.mean(e, axis=-1, keepdims=True) - x * jnp.mean(e * x, axis=-1, keepdims=True))
+    g_out[...] = jnp.where(live_rows(ROWS), g_in[...].astype(F32) + inner, 0.0).astype(BF16)
+
+
+def chain_scratch():
+    V = pltpu.VMEM
+    mixer = [V((ROWS, W), F32), V((ROWS, 1), F32), V((ROWS, W), BF16), V((ROWS, 3 * W), BF16)]
+    feed = [V((ROWS, W), F32), V((ROWS, 1), F32), V((ROWS, W), BF16), V((ROWS, 4 * W), F32)]
+    return (mixer + [V((6, 8, PAIR, PAIR), F32), V((ROWS, W), BF16)] + feed + mixer + [V((6, 4, LANES, LANES), F32), V((ROWS, W), BF16)] + feed
+            + [V((ROWS, W), F32), V((ROWS, W), F32), V((ROWS, W), BF16), V((ROWS, 3 * W), BF16), V((PAIR, PAIR), F32), V((LANES, LANES), F32)])
+
+
+def fill_biases(win_bias, chan_bias):
+    qi = lax.broadcasted_iota(jnp.int32, (PAIR, PAIR), 0)
+    ki = lax.broadcasted_iota(jnp.int32, (PAIR, PAIR), 1)
+    win_bias[...] = jnp.where(((qi // IMG) == (ki // IMG)) & (lax.rem(ki, IMG) < LIVE), 0.0, -1e30).astype(F32)
+    ci = lax.broadcasted_iota(jnp.int32, (LANES, LANES), 0)
+    ei = lax.broadcasted_iota(jnp.int32, (LANES, LANES), 1)
+    chan_bias[...] = jnp.where((ci // HD) == (ei // HD), 0.0, -1e30).astype(F32)
+
+
+class Chain:
+    def __init__(self, w, small, mask, u, g, sg, dw, scratch):
+        self.w, self.small, self.mask, self.u, self.g, self.sg, self.dw = w, small, mask, u, g, sg, dw
+        s = scratch
+        self.window, self.feed0, self.channel, self.feed1 = s[0:6], s[6:10], s[10:16], s[16:20]
+        self.c_ref, self.acc, self.dm, self.dt, self.win_bias, self.chan_bias = s[20:26]
+
+    def forward(self, k):
+        u, w, small = self.u, self.w, self.small
+        if k == 0:
+            fill_biases(self.win_bias, self.chan_bias)
+            mix_forward(0, False, u[0], u[1], w, small, self.mask, self.win_bias, self.c_ref, *self.window)
+        if k == 1:
+            ff_forward(0, u[1], u[2], w, small, *self.feed0, self.acc)
+        if k == 2:
+            mix_forward(1, True, u[2], u[3], w, small, self.mask, self.chan_bias, self.c_ref, *self.channel)
+        if k == 3:
+            ff_forward(1, u[3], u[4], w, small, *self.feed1, self.acc)
+
+    def backward(self, k):
+        u, g, w, small, sg = self.u, self.g, self.w, self.small, self.sg
+        if k in (0, 2):
+            parts = self.channel if k == 2 else self.window
+            mix_backward(k // 2, k == 2, u[k], g[k + 1], g[k], w, small, self.mask, sg, self.dw, self.c_ref, *parts, self.dm, self.dt, self.acc)
+        else:
+            x, r, _, slope = self.feed0 if k == 1 else self.feed1
+            ff_backward(k // 2, g[k + 1], g[k], w, small, sg, x, r, slope, self.acc)
+
+
+MESH = pl.DeviceIdType.MESH
+STRIP = 96
+
+
+def slot(item, line, d):
+    red = lax.rem(item, 3) // 2
+    block = 12 * (item // 3) + 4 * lax.rem(item, 3) + (1 - red) * line + red * (d // 2)
+    row = (1 - red) * STRIP * d + red * (4 * STRIP * lax.rem(d, 2) + STRIP * line)
+    return block, row
+
+
+def other_planes(z):
+    near = z + 1 - 2 * (z // 2)
+    far = 3 * (1 - z // 2)
+    return near, 6 - z - near - far, far
+
+
+class Place:
+    def __init__(self):
+        self.s = lax.axis_index("segment")
+        self.d = lax.axis_index("dp")
+        self.z = self.d // 2
+        self.c = lax.rem(self.d, 2)
+        self.xn = self.s + 1 - 2 * lax.rem(self.s, 2)
+        self.yn = lax.rem(self.s + 2, 4)
+        self.dn = 3 - self.s
+        self.twin = self.d + 1 - 2 * self.c
+
+
+def greet_neighbours(at):
+    bar = pltpu.get_barrier_semaphore()
+
+    def greet(seg, dev):
+        pl.semaphore_signal(bar, inc=1, device_id=(seg, dev), device_id_type=MESH)
+
+    greet(at.xn, at.d)
+    greet(at.yn, at.d)
+    greet(at.s, at.twin)
+
+    @pl.when(at.z < 3)
+    def _():
+        greet(at.s, at.d + 2)
+
+    @pl.when(at.z > 0)
+    def _():
+        greet(at.s, at.d - 2)
+
+    pl.semaphore_wait(bar, 4 + (at.z * (3 - at.z)) // 2)
+
+
+def remote(src, dst, ssem, rsem, seg, dev):
+    return pltpu.make_async_remote_copy(src, dst, ssem, rsem, device_id=(seg, dev), device_id_type=MESH)
+
+
+def gather_scratch():
+    D = pltpu.SemaphoreType.DMA
+    return [D((2, 9)), D((6, 5)), D((6, 3, 2)), D((6, 3, 2)), D((6, 4, 4)), D((2, 3, 4)), D((2, 3, 4))]
+
+
+class Gather:
+    def __init__(self, at, shards, wbuf, sems):
+        self.at, self.shards, self.w = at, shards, wbuf
+        self.lsem, self.zs, self.xs, self.ys, self.pr, self.cs, self.cr = sems
+        self.planes = other_planes(at.z)
+        self.away = 2 * (at.z // 2) - 1
+        self.inner = (at.z == 1) | (at.z == 2)
+        self.groups = [(layer, part, k) for layer in range(2) for part in range(3) for k in range(3)]
+
+    def strip(self, item, line, plane):
+        block, row = slot(item, line, 2 * plane + self.at.c)
+        return self.w.at[block, pl.ds(pl.multiple_of(row, STRIP), STRIP), :]
+
+    def quad_ref(self, layer, part, plane, core):
+        if part == 2:
+            return self.w.at[12 * layer + 8 + plane, pl.ds(pl.multiple_of(4 * STRIP * core, 4 * STRIP), 4 * STRIP), :]
+        row = pl.multiple_of(STRIP * (2 * plane + core), STRIP)
+        return self.w.at[pl.ds(12 * layer + 4 * part, 4), pl.ds(row, STRIP), :]
+
+    def quad(self, layer, part, plane, core, k):
+        ref = self.quad_ref(layer, part, plane, core)
+        return remote(ref, ref, self.cs.at[layer, part, k], self.cr.at[layer, part, plane], self.at.s, self.at.twin)
+
+    def local(self, layer):
+        triple, output, expand, reduce = self.shards
+        at, w, base = self.at, self.w, 12 * layer
+        rows = pl.ds(pl.multiple_of(STRIP * at.d, STRIP), STRIP)
+        sems = self.lsem.at
+        copies = [pltpu.make_async_copy(triple.at[layer, :, pl.ds(W * j, W)], w.at[base + j, rows, :], sems[layer, j]) for j in range(3)]
+        copies.append(pltpu.make_async_copy(output.at[layer], w.at[base + 3, rows, :], sems[layer, 3]))
+        copies += [pltpu.make_async_copy(expand.at[layer, :, pl.ds(W * j, W)], w.at[base + 4 + j, rows, :], sems[layer, 4 + j]) for j in range(4)]
+        half = pl.ds(pl.multiple_of(4 * STRIP * at.c, 4 * STRIP), 4 * STRIP)
+        copies.append(pltpu.make_async_copy(reduce.at[layer], w.at[base + 8 + at.z, half, :], sems[layer, 8]))
+        return copies
+
+    def up(self, item):
+        ref = self.strip(item, self.at.s, self.at.z)
+        return remote(ref, ref, self.zs.at[item, 0], self.pr.at[item, self.at.z, self.at.s], self.at.s, self.at.d + 2)
+
+    def down(self, item):
+        ref = self.strip(item, self.at.s, self.at.z)
+        return remote(ref, ref, self.zs.at[item, 1], self.pr.at[item, self.at.z, self.at.s], self.at.s, self.at.d - 2)
+
+    def onward(self, item, k):
+        step = self.away if k != 1 else -self.away
+        ref = self.strip(item, self.at.s, self.planes[k])
+        return remote(ref, ref, self.zs.at[item, 2 + k], self.pr.at[item, self.planes[k], self.at.s], self.at.s, self.at.d + 2 * step)
+
+    def to_x(self, item, k, line, j):
+        ref = self.strip(item, line, self.planes[k])
+        return remote(ref, ref, self.xs.at[item, k, j], self.pr.at[item, self.planes[k], line], self.at.xn, self.at.d)
+
+    def to_y(self, item, k, line, j):
+        ref = self.strip(item, line, self.planes[k])
+        return remote(ref, ref, self.ys.at[item, k, j], self.pr.at[item, self.planes[k], line], self.at.yn, self.at.d)
+
+    def arrival(self, item, k, line):
+        ref = self.strip(item, line, self.planes[k])
+        return remote(ref, ref, self.zs.at[item, 0], self.pr.at[item, self.planes[k], line], self.at.s, self.at.twin)
+
+    def ends(self, item, act):
+        @pl.when(self.at.z < 3)
+        def _():
+            act(self.up(item))
+
+        @pl.when(self.at.z > 0)
+        def _():
+            act(self.down(item))
+
+    def begin(self):
+        at = self.at
+        copies = [self.local(layer) for layer in range(2)]
+        for layer in range(2):
+            for copy in copies[layer]:
+                copy.start()
+        for copy in copies[0]:
+            copy.wait()
+        self.ends(0, lambda copy: copy.start())
+        for part in range(3):
+            self.quad(0, part, at.z, at.c, 3).start()
+        for copy in copies[1]:
+            copy.wait()
+        for part in range(3):
+            self.quad(1, part, at.z, at.c, 3).start()
+
+    def stage_a(self, layer, part, k):
+        item = 3 * layer + part
+        self.arrival(item, k, self.at.s).wait_recv()
+
+        @pl.when(self.inner)
+        def _():
+            self.onward(item, k).start()
+
+        self.to_x(item, k, self.at.s, 0).start()
+        self.to_y(item, k, self.at.s, 0).start()
+
+    def stage_b(self, layer, part, k):
+        item = 3 * layer + part
+        self.arrival(item, k, self.at.xn).wait_recv()
+        if (part + k + layer) % 2 == 0:
+            self.to_y(item, k, self.at.xn, 1).start()
+        self.arrival(item, k, self.at.yn).wait_recv()
+        if (part + k + layer) % 2 == 1:
+            self.to_x(item, k, self.at.yn, 1).start()
+
+    def stage_c(self, layer, part, k):
+        item = 3 * layer + part
+        self.arrival(item, k, self.at.dn).wait_recv()
+        self.quad(layer, part, self.planes[k], self.at.c, k).start()
+
+    def step(self, g):
+        n = len(self.groups)
+        if g < n and g % 3 == 0 and g // 3 + 1 < 6:
+            self.ends(g // 3 + 1, lambda copy: copy.start())
+        if g < n:
+            self.stage_a(*self.groups[g])
+        if 0 <= g - 1 < n:
+            self.stage_b(*self.groups[g - 1])
+        if 0 <= g - 2 < n:
+            self.stage_c(*self.groups[g - 2])
+
+    def settle(self, layer, part):
+        for k in range(3):
+            self.quad(layer, part, self.planes[k], 1 - self.at.c, k).wait_recv()
+        self.quad(layer, part, self.at.z, 1 - self.at.c, 3).wait_recv()
+
+    def drain(self):
+        at = self.at
+        for layer in range(2):
+            for part in range(3):
+                item = 3 * layer + part
+                self.ends(item, lambda copy: copy.wait_send())
+                self.quad(layer, part, at.z, at.c, 3).wait_send()
+                for k in range(3):
+                    @pl.when(self.inner)
+                    def _():
+                        self.onward(item, k).wait_send()
+
+                    self.to_x(item, k, at.s, 0).wait_send()
+                    self.to_y(item, k, at.s, 0).wait_send()
+                    if (part + k + layer) % 2 == 0:
+                        self.to_y(item, k, at.xn, 1).wait_send()
+                    else:
+                        self.to_x(item, k, at.yn, 1).wait_send()
+                    self.quad(layer, part, self.planes[k], at.c, k).wait_send()
+
+
+def chain_kernel(triple, output, expand, reduce, small, x, mask, gin, u_out, g_out, sg, w_out, w, osem, *scratch):
+    at = Place()
+    gather = Gather(at, (triple, output, expand, reduce), w, scratch[:7])
+    u = [x] + [u_out.at[i] for i in range(4)]
+    g = [g_out.at[i] for i in range(4)] + [gin]
+
+    def dw(layer, j, lhs, rhs):
+        w[12 * layer + j] = mm_tn(lhs[...], rhs()).astype(BF16)
+
+    chain = Chain(w, small, mask, u, g, sg, dw, scratch[7:])
+    sg[...] = jnp.zeros_like(sg)
+    greet_neighbours(at)
+    gather.begin()
+    for step in range(20):
+        gather.step(step)
+    for layer in range(2):
+        for part in range(3):
+            gather.settle(layer, part)
+    gather.drain()
+    for k in range(4):
+        chain.forward(k)
+    for k in (3, 2, 1, 0):
+        chain.backward(k)
+    keep = pltpu.make_async_copy(w, w_out, osem)
+    keep.start()
+    keep.wait()
+
+
+def chain_call(triple, output, expand, reduce, small, x, mask, gin):
+    V = pltpu.VMEM
+    S = jax.ShapeDtypeStruct
+    anywhere = pl.BlockSpec(memory_space=pl.ANY)
+    vmem = pl.BlockSpec(memory_space=V)
+    return pl.pallas_call(
+        chain_kernel,
+        out_shape=(S((4, ROWS, W), BF16), S((4, ROWS, W), BF16), S((2, 24, W), F32), S((24, W, W), BF16)),
+        in_specs=[anywhere] * 4 + [vmem] * 4,
+        out_specs=[vmem] * 3 + [anywhere],
+        scratch_shapes=[V((24, W, W), BF16), pltpu.SemaphoreType.DMA] + gather_scratch() + chain_scratch(),
+        compiler_params=pltpu.CompilerParams(collective_id=1, has_side_effects=True, vmem_limit_bytes=63 * 1024 * 1024),
+        name="gather_and_chain",
+    )(triple, output, expand, reduce, small, x, mask, gin)
+
+
+def pack_small(conv_weight, conv_bias, mixer_gain, mixer_shift, triple_bias, output_bias, feed_gain, feed_shift, expand_bias, reduce_bias):
+    part = conv_bias.shape[1]
+    rows = [conv_weight] + [
+        v.reshape(2, -1, part)
+        for v in (conv_bias, mixer_gain, mixer_shift, triple_bias, output_bias, feed_gain, feed_shift, expand_bias, reduce_bias)
+    ]
+    return jnp.concatenate(rows, axis=1)
+
+
+def spread_small(packed):
+    n = packed.shape[0]
+
+    def rows(lo, hi):
+        return jnp.transpose(packed[:, :, lo:hi], (1, 2, 0, 3)).reshape(2, hi - lo, W)
+
+    def long(lo, hi):
+        return jnp.transpose(packed[:, :, lo:hi], (1, 0, 2, 3)).reshape(2, hi - lo, W)
+
+    zero = jnp.zeros((2, 1, W), packed.dtype)
+    return jnp.concatenate([rows(0, 12), long(12, 15), rows(15, 18), long(18, 22), rows(22, 23), zero], axis=1)
+
+
+def pad_images(rows):
+    return jnp.pad(rows.reshape(-1, LIVE, rows.shape[1]), ((0, 0), (0, IMG - LIVE), (0, 0))).reshape(-1, rows.shape[1])
+
+
+def unpad_images(rows):
+    lead = rows.shape[:-2]
+    return rows.reshape(lead + (-1, IMG, W))[..., :LIVE, :].reshape(lead + (-1, W))
+
+
+def spread_body(
+    patches, region_mask, conv_weight, conv_bias, mixer_gain, mixer_shift, triple_weight, triple_bias, output_weight,
+    output_bias, feed_gain, feed_shift, expand_weight, expand_bias, reduce_weight, reduce_bias, cotangent,
+):
+    s = lax.axis_index("segment")
+    d = lax.axis_index("dp")
+    packed = pack_small(conv_weight, conv_bias, mixer_gain, mixer_shift, triple_bias, output_bias, feed_gain, feed_shift, expand_bias, reduce_bias)
+    small = spread_small(lax.all_gather(packed, "dp", axis=0)).astype(F32)
+    own = patches.shape[0] // lax.axis_size("segment")
+    mine = lambda v: lax.dynamic_slice_in_dim(v, s * own, own, 0)
+    x = pad_images(mine(patches))
+    gin = pad_images(mine(cotangent))
+    mask = pad_images(mine(region_mask).astype(BF16)[:, None])
+    u, g, sg, w = chain_call(triple_weight, output_weight, expand_weight, reduce_weight, small, x, mask, gin)
+    sections = lambda v: lax.all_to_all(unpad_images(v), "segment", split_axis=0, concat_axis=1, tiled=True)
+    blocks = []
+    for layer in range(2):
+        e_w, r_w = w[12 * layer + 4:12 * layer + 8], w[12 * layer + 8:12 * layer + 12]
+        ui = u[2 * layer].astype(F32)
+        go = g[2] if layer == 0 else gin
+        hat, _ = norm_parts(ui)
+        n = (hat * small[layer, 16] + small[layer, 17]).astype(BF16)
+        es, rs = [], []
+        for j in range(4):
+            h = mm(n, e_w[j]) + small[layer, 18 + j]
+            a, pull = jax.vjp(gelu_exact, h)
+            dh = pull(mm_nt(go, r_w[j]))[0].astype(BF16)
+            es.append(mm_tn(n, dh).astype(BF16))
+            rs.append(mm_tn(a.astype(BF16), go).astype(BF16))
+        blocks.append((w[12 * layer:12 * layer + 4], jnp.stack(es), jnp.stack(rs)))
+    dp = lax.axis_size("dp")
+    by_row = lambda v: v.reshape(4, dp, W // dp, W).transpose(1, 2, 0, 3)
+    total = jnp.concatenate(
+        [jnp.concatenate([by_row(m).reshape(dp, -1, W), by_row(e).reshape(dp, -1, W), r.reshape(dp, -1, W)], axis=1) for m, e, r in blocks], axis=1
+    )
+    total = lax.psum_scatter(total, "dp", scatter_dimension=0, tiled=True)[0]
+    total = lax.psum(total, "segment").astype(F32)
+    part = W // dp
+    total = total.reshape(2, 3, part * 4, W)
+    mix = total[:, 0].reshape(2, part, 4 * W)
+    exp = total[:, 1].reshape(2, part, 4 * W)
+    red = total[:, 2]
+    sg = lax.psum(sg, ("segment", "dp"))
+    cut = lambda lo, hi: lax.dynamic_slice_in_dim(sg[:, lo:hi].reshape(2, -1), d * part * (hi - lo), part * (hi - lo), 1)
+    taps = lax.dynamic_slice_in_dim(sg[:, :9], d * part, part, 2)
+    return (
+        sections(u), sections(g), taps, cut(9, 10), cut(10, 11), cut(11, 12), mix[:, :, :3 * W], cut(12, 15), mix[:, :, 3 * W:],
+        cut(15, 16), cut(16, 17), cut(17, 18), exp, cut(18, 22), red, cut(22, 23),
+    )
+
+
 def solution(mesh):
     in_specs = (
         P("dp", None),
@@ -553,4 +1173,5 @@
         P(None, "dp", None),
         P(None, "dp"),
     )
-    return jax.shard_map(body, mesh=mesh, in_specs=in_specs, out_specs=out_specs, check_vma=False)
+    chosen = spread_body if mesh.shape["dp"] == 8 and mesh.shape["segment"] == 4 else body
+    return jax.shard_map(chosen, mesh=mesh, in_specs=in_specs, out_specs=out_specs, check_vma=False)

time: 1730 us -> 817 us (0.47)
  local copies, waits for them, and re-layouts: 388 us -> 105 us
  loops' own time: 280 us -> 0 us
  other arithmetic: 212 us -> 7.04 us
  Pallas kernels: 0 us -> 173 us
  waiting for transfers between devices: 556 us -> 414 us
  blocking collectives: 90.1 us -> 12.1 us
  matrix products: 145 us -> 75.4 us
  starting transfers between devices: 28.8 us -> 7.56 us
    another operation x14 -> x0, loops' own time: 280 us -> none  [the longest x7 162 us: run_segments(): lax.switch(jnp.where(is_live, segment_index, segments), backward_branches...]
    ppermute x12 -> x0, waiting for transfers between devices: 181 us -> none  [shifted_2(): return lax.ppermute(x, axis, pairs)]
    pallas_call x0 -> x1, Pallas kernels: none -> 173 us  [chain_call(): pl.pallas_call(chain_kernel, out_shape=(S((4, ROWS, W), BF16), S((4, ROWS...]
    all_gather x4 -> x0, waiting for transfers between devices: 115 us -> none  [the longest x1 52.8 us: body(): lax.all_gather(slices[10], 'dp', axis=0, tiled=True)]
    reduce_scatter x4 -> x1, waiting for transfers between devices: 180 us -> 281 us  [spread_body(): total = lax.psum_scatter(total, 'dp', scatter_dimension=0, tiled=True)[0]]
    add x22 -> x0, other arithmetic: 88.8 us -> none  [the longest x14 82.2 us: run_segments(): first_term + second_term]
    another operation x79 -> x7, local copies, waits for them, and re-layouts: 87.8 us -> 10 us  [the longest x4 3.88 us: spread_body(): blocks.append((w[12 * layer:12 * layer + 4], jnp.stack(es), jnp.stack(rs)))]
    dot_general x60 -> x24, matrix products: 145 us -> 75.4 us  [the longest x16 61.1 us: mm_tn(): lax.dot_general(a, b, (((0,), (0,)), ((), ())), preferred_element_type=F32)]
  transfers between devices with their start and end apart: 22 -> 5, of which waited for: 18 -> 4; matrix products, arithmetic and copies ran while one was open for 9% -> 2% of each run, Pallas kernels for 0% -> 0%
where the time goes in v1:
time: 817 us; the launch traced here: 810 us
  waiting for transfers between devices  414 us (51%)
  Pallas kernels  173 us (21%)
  local copies, waits for them, and re-layouts  105 us (13%)
  matrix products  75.4 us (9%)
  between operations  16.3 us (2%)
  blocking collectives  12.1 us (1%)
    reduce_scatter x1, waiting for transfers between devices, spread_body(): total = lax.psum_scatter(total, 'dp', scatter_dimension=0, tiled=True)[0]  281 us
    pallas_call x1, Pallas kernels, chain_call(): pl.pallas_call(chain_kernel, out_shape=(S((4, ROWS, W), BF16), S((4, ROWS...  173 us
    psum x1, waiting for transfers between devices, spread_body(): total = lax.psum(total, 'segment').astype(F32)  71.1 us
    dot_general x16, matrix products, mm_tn(): lax.dot_general(a, b, (((0,), (0,)), ((), ())), preferred_element_type=F32)  61.1 us
    psum x1, waiting for transfers between devices, spread_body(): sg = lax.psum(sg, ('segment', 'dp'))  41.3 us
    concatenate x2, local copies, waits for them, and re-layouts, spread_body(): jnp.concatenate([jnp.concatenate([by_row(m).reshape(dp, -1, W), by_row(e)...  24.3 us
    unnamed x63, local copies, waits for them, and re-layouts  23.5 us
    all_to_all x2, waiting for transfers between devices, spread_body(): lax.all_to_all(unpad_images(v), 'segment', split_axis=0, concat_axis=1, t...  20.6 us
  transfers between devices with their start and end apart: 5, of which 4 were waited for; matrix products, arithmetic and copies ran while one was open for 2% of the time, Pallas kernels for 0%

profile of v1, /device:TPU:16, one launch (start us, length us, event | category | flops | bytes accessed | tf_op | source)
XLA Modules:
  0.0 809.8 jit_solution(4813568669239448137)
XLA Ops:
  15.0 12.1 %all-gather = bf16[16,23,96]{2,1,0:T(8,128)(2,1)S(1)} all-gather(bf16[2,23,96]{2,1,0:T(8,128)(2,1)S(1)} %concatenate.11), channel_id=2, replica_groups=mesh['segment'=4,'dp'=8] {'dp'}, dimensions={0}, use_global_device_ids=true | all-gather | bytes 79488 | tf_op jit(solution)/shard_map/all_gather | solution.py:1094
  32.7 172.5 %gather_and_chain.1 = (bf16[4,224,768]{2,1,0:T(8,128)(2,1)}, bf16[4,224,768]{2,1,0:T(8,128)(2,1)}, f32[2,24,768]{2,1,0:T(8,128)}, bf16[24,768,768]{2,1,0:T(8,128)(2,1)}) custom-call(bf16[2,96,2304]{2,1,0:T(8,128)(2,1)} %triple.1, bf16[2,96,768]{2,1,0:T(8,128)(2,1)} %output.1, bf16[2,96,3072]{2,1,0:T(8,128)(2,1)} %expand.1, bf16[2,384,768]{2,1,0:T(8,128)(2,1)} %reduce.27, ...), custom_call_target="tpu_custom_call" | custom-call | tf_op jit(solution)/shard_map/gather_and_chain/pallas_call | solution.py:1045
  209.9 3.0 fusion.4
  212.9 4.7 convolution_convert_fusion.7
  219.4 3.0 fusion.7
  222.3 4.9 convolution_convert_fusion.4
  229.1 2.9 fusion.6
  232.0 4.7 convolution_convert_fusion.5
  238.5 4.7 convolution_convert_fusion.6
  243.2 3.0 fusion.5
  248.1 3.2 fusion
  251.2 4.7 convolution_convert_fusion.15
  257.7 2.9 fusion.3
  260.6 4.7 convolution_convert_fusion.12
  267.1 3.0 fusion.2
  270.1 5.1 convolution_convert_fusion.13
  275.2 8.0 fusion.288
  284.9 4.7 convolution_convert_fusion.14
  300.8 2.6 copy.113
  308.8 2.7 constant_dynamic-update-slice_fusion.2
  313.0 4.8 copy_dynamic-update-slice_fusion.1
  320.3 2.7 constant_dynamic-update-slice_fusion
  325.0 4.8 copy_dynamic-update-slice_fusion
  329.8 19.5 %copy.122 = bf16[8,2304,768]{2,1,0:T(8,128)(2,1)} copy(bf16[8,2304,768]{2,0,1:T(8,128)(2,1)} %copy_dynamic-update-slice_fusion) | data formatting | bytes 56623104 | tf_op jit(solution)/shard_map/concatenate | solution.py:1119
  349.9 280.5 %reduce-scatter.2.cloned.1.call-done = bf16[1,2304,768]{2,1,0:T(8,128)(2,1)} async-done(((bf16[8,2304,768]{2,1,0:T(8,128)(2,1)}), bf16[1,2304,768]{2,1,0:T(8,128)(2,1)}) %reduce-scatter.2.cloned.1.call-update) | async-done | bytes 3538960 | tf_op jit(solution)/shard_map/reduce_scatter | solution.py:1122
  632.5 3.6 all-to-all-start
  638.3 41.3 %all-reduce.6.cloned.1.call-done = f32[2,24,768]{2,1,0:T(8,128)} async-done(((f32[2,24,768]{2,1,0:T(8,128)}), f32[2,24,768]{2,1,0:T(8,128)}) %all-reduce.6.cloned.1.call-update) | async-done | bytes 147472 | tf_op jit(solution)/shard_map/psum | solution.py:1129
  683.2 3.8 all-to-all-start.1
  694.5 20.6 %all-to-all-done.1 = bf16[4,196,768]{2,1,0:T(8,128)(2,1)S(1)} async-done(((bf16[4,196,768]{2,1,0:T(8,128)(2,1)}), bf16[4,196,768]{2,1,0:T(8,128)(2,1)S(1)}, u32[]{:S(2)}, u32[]{:S(2)}) %all-to-all-start.1) | async-done | bytes 1204256 | tf_op jit(solution)/shard_map/all_to_all | solution.py:1101
  716.3 71.1 %all-reduce.8.cloned.1.call-done = bf16[2,3,384,768]{3,2,1,0:T(8,128)(2,1)} async-done(((bf16[2,3,384,768]{3,2,1,0:T(8,128)(2,1)}), bf16[2,3,384,768]{3,2,1,0:T(8,128)(2,1)}) %all-reduce.8.cloned.1.call-update) | async-done | bytes 3538960 | tf_op jit(solution)/shard_map/psum | solution.py:1123
  787.4 4.2 fusion.289
  796.4 3.5 reshape_squeeze.7
  (149 shorter events, 75.9 us)
Async XLA Ops:
  8.0 622.4 %reduce-scatter.2.cloned.1.call-start = ((), (), s32[]{:S(2)}) async-start(), calls=%async_computation.4 | async-start | bytes 31850496 | tf_op jit(solution)/shard_map/reduce_scatter | solution.py:1122
  29.7 2.3 copy-start.18
  205.3 2.8 copy-start.1
  208.1 1.8 copy-start.3
  246.2 1.9 copy-start.2
  289.6 1.9 copy-start.9
  289.6 1.9 copy-start.11
  289.6 2.0 copy-start.13
  289.6 2.3 copy-start.14
  292.0 6.2 slice-start.2
  292.8 2.7 copy-start.15
  292.8 5.4 slice-start.3
  295.4 1.3 copy-start.16
  296.1 1.4 copy-start.17
  298.1 2.7 slice-start
  298.2 2.7 slice-start.1
  308.7 2.7 copy-start.8
  308.7 2.7 copy-start.10
  308.8 3.7 copy-start.12
  320.3 2.7 copy-start.4
  320.3 2.7 copy-start.5
  320.3 3.7 copy-start.6
  320.3 4.0 copy-start.7
  349.3 330.3 %all-reduce.6.cloned.1.call-start = ((), (), s32[]{:S(2)}) async-start(), calls=%async_computation.3 | async-start | bytes 294912 | tf_op jit(solution)/shard_map/psum | solution.py:1129
  349.8 437.6 %all-reduce.8.cloned.1.call-start = ((), (), s32[]{:S(2)}) async-start(), calls=%async_computation.5 | async-start | bytes 7077888 | tf_op jit(solution)/shard_map/psum | solution.py:1123
  632.5 50.7 %all-to-all-start = ((bf16[4,196,768]{2,1,0:T(8,128)(2,1)}), bf16[4,196,768]{2,1,0:T(8,128)(2,1)S(1)}, u32[]{:S(2)}, u32[]{:S(2)}) async-start(bf16[4,196,768]{2,1,0:T(8,128)(2,1)} %copy.110), calls=%async_computation | async-start | bytes 2457600 | tf_op jit(solution)/shard_map/all_to_all | solution.py:1101
  683.2 31.9 %all-to-all-start.1 = ((bf16[4,196,768]{2,1,0:T(8,128)(2,1)}), bf16[4,196,768]{2,1,0:T(8,128)(2,1)S(1)}, u32[]{:S(2)}, u32[]{:S(2)}) async-start(bf16[4,196,768]{2,1,0:T(8,128)(2,1)} %copy.112), calls=%async_computation.1 | async-start | bytes 2457600 | tf_op jit(solution)/shard_map/all_to_all | solution.py:1101
  796.4 3.5 copy-start
Sparse Core Ops, SparseCore 0:
  349.4 280.9 reduce-scatter.1
Sparse Core Ops, SparseCore 1:
  355.3 324.3 all-reduce.5
  682.6 104.7 all-reduce.7

commit v2 on v1

--- a/solution.py
+++ b/solution.py
@@ -1009,7 +1009,7 @@
                     self.quad(layer, part, self.planes[k], at.c, k).wait_send()
 
 
-def chain_kernel(triple, output, expand, reduce, small, x, mask, gin, u_out, g_out, sg, w_out, w, osem, *scratch):
+def chain_kernel(triple, output, expand, reduce, small, x, mask, gin, u_out, g_out, sg, mix_out, fw_out, w, osem, *scratch):
     at = Place()
     gather = Gather(at, (triple, output, expand, reduce), w, scratch[:7])
     u = [x] + [u_out.at[i] for i in range(4)]
@@ -1032,9 +1032,13 @@
         chain.forward(k)
     for k in (3, 2, 1, 0):
         chain.backward(k)
-    keep = pltpu.make_async_copy(w, w_out, osem)
-    keep.start()
-    keep.wait()
+    lay, quarter = at.s // 2, 2 * lax.rem(at.s, 2) + at.c
+    keep = [pltpu.make_async_copy(w.at[pl.ds(12 * i, 4)], mix_out.at[pl.ds(4 * i, 4)], osem.at[i]) for i in range(2)]
+    keep += [pltpu.make_async_copy(w.at[12 * lay + 4 + 4 * i + quarter], fw_out.at[i], osem.at[2 + i]) for i in range(2)]
+    for copy in keep:
+        copy.start()
+    for copy in keep:
+        copy.wait()
 
 
 def chain_call(triple, output, expand, reduce, small, x, mask, gin):
@@ -1044,13 +1048,407 @@
     vmem = pl.BlockSpec(memory_space=V)
     return pl.pallas_call(
         chain_kernel,
-        out_shape=(S((4, ROWS, W), BF16), S((4, ROWS, W), BF16), S((2, 24, W), F32), S((24, W, W), BF16)),
+        out_shape=(S((4, ROWS, W), BF16), S((4, ROWS, W), BF16), S((2, 24, W), F32), S((8, W, W), BF16), S((2, W, W), BF16)),
         in_specs=[anywhere] * 4 + [vmem] * 4,
-        out_specs=[vmem] * 3 + [anywhere],
-        scratch_shapes=[V((24, W, W), BF16), pltpu.SemaphoreType.DMA] + gather_scratch() + chain_scratch(),
+        out_specs=[vmem] * 3 + [anywhere] * 2,
+        scratch_shapes=[V((24, W, W), BF16), pltpu.SemaphoreType.DMA((4,))] + gather_scratch() + chain_scratch(),
         compiler_params=pltpu.CompilerParams(collective_id=1, has_side_effects=True, vmem_limit_bytes=63 * 1024 * 1024),
         name="gather_and_chain",
     )(triple, output, expand, reduce, small, x, mask, gin)
+
+
+def greet_all(at):
+    bar = pltpu.get_barrier_semaphore()
+
+    def greet(seg, dev):
+        pl.semaphore_signal(bar, inc=1, device_id=(seg, dev), device_id_type=MESH)
+
+    for seg in (at.xn, at.yn, at.dn):
+        greet(seg, at.d)
+        greet(seg, at.twin)
+    greet(at.s, at.twin)
+    greet(at.s, lax.rem(at.d + 4, 8))
+
+    @pl.when(at.z < 3)
+    def _():
+        greet(at.s, at.d + 2)
+
+    @pl.when(at.z > 0)
+    def _():
+        greet(at.s, at.d - 2)
+
+    pl.semaphore_wait(bar, 9 + (at.z * (3 - at.z)) // 2)
+
+
+def add_into(total, term):
+    total[...] = (total[...].astype(F32) + term[...].astype(F32)).astype(BF16)
+
+
+class PlaneSum:
+    def __init__(self, at, below, above, ssem, bsem, asem):
+        self.at, self.below, self.above, self.ssem, self.bsem, self.asem = at, below, above, ssem, bsem, asem
+
+    def up(self, i, ref):
+        return remote(ref, self.below.at[i], self.ssem.at[i], self.bsem.at[i], self.at.s, self.at.d + 2)
+
+    def down(self, i, ref):
+        return remote(ref, self.above.at[i], self.ssem.at[i], self.asem.at[i], self.at.s, self.at.d - 2)
+
+    def from_below(self, i, ref):
+        @pl.when(self.at.z > 0)
+        def _():
+            self.up(i, ref).wait_recv()
+            add_into(ref, self.below.at[i])
+
+    def from_above(self, i, ref):
+        @pl.when(self.at.z < 3)
+        def _():
+            self.down(i, ref).wait_recv()
+            add_into(ref, self.above.at[i])
+
+    def step(self, i, ref, goal):
+        z = self.at.z
+
+        @pl.when(z <= goal)
+        def _():
+            self.from_below(i, ref)
+
+        @pl.when(z >= goal)
+        def _():
+            self.from_above(i, ref)
+
+        @pl.when(z < goal)
+        def _():
+            self.up(i, ref).start()
+
+        @pl.when(z > goal)
+        def _():
+            self.down(i, ref).start()
+
+    def drain(self, i, ref, goal):
+        @pl.when(self.at.z < goal)
+        def _():
+            self.up(i, ref).wait_send()
+
+        @pl.when(self.at.z > goal)
+        def _():
+            self.down(i, ref).wait_send()
+
+
+def goal_order(z):
+    far = 3 * (1 - z // 2)
+    near = 2 - z // 2
+    return far, near, 6 - far - near - z, z
+
+
+UNITS = [("mix", layer, j) for layer in range(2) for j in range(4)]
+UNITS += [("exp", layer, j) for layer in range(2) for j in range(4)]
+UNITS += [("red", layer, j) for layer in range(2) for j in range(2)]
+
+
+def sum_kernel(u, g, cot, mix, fw, small, sg, sec_out, grad_out, fin, sg_out,
+               xin, gin, nbuf, abuf, dhbuf, fwv, dwe, dwr, mown, mrx, prx, below_m, above_m, below_f, above_f, sgr, sga,
+               lsem, xsend, xrecv, gsend, grecv, tws, twr, osend, orecv, msend, mrecv, psend, precv,
+               zms, zmb, zma, zfs, zfb, zfa, fsend, frecv, sgs, sgv):
+    at = Place()
+    s, d, z, c = at.s, at.d, at.z, at.c
+    lay = s // 2
+    quarter = 2 * lax.rem(s, 2) + c
+    segs = (at.xn, at.yn, at.dn)
+    greet_all(at)
+
+    weights = pltpu.make_async_copy(fw, fwv, lsem.at[0])
+    weights.start()
+    strips = []
+    for p in range(4):
+        rows = pl.ds(pl.multiple_of(2 * STRIP * p + STRIP * c, STRIP), STRIP)
+        strips.append(pltpu.make_async_copy(mix.at[:, rows, :], mown.at[:, p], lsem.at[1 + p]))
+        strips[-1].start()
+    seeds = [pltpu.make_async_copy(cot.at[t], gin.at[2 * t + c], lsem.at[5 + t]) for t in range(4)]
+
+    @pl.when(s >= 2)
+    def _():
+        for copy in seeds:
+            copy.start()
+
+    def x_send(i):
+        t = segs[i]
+        return remote(u.at[2 * (t // 2)], xin.at[2 * s + c], xsend.at[i], xrecv.at[s], t, d)
+
+    def g_send(i):
+        return remote(g.at[2], gin.at[2 * s + c], gsend.at[i], grecv.at[s], segs[i], d)
+
+    def x_arrival(t):
+        return remote(xin.at[2 * t + c], xin.at[2 * t + c], xsend.at[0], xrecv.at[t], s, at.twin)
+
+    def g_arrival(t):
+        return remote(gin.at[2 * t + c], gin.at[2 * t + c], gsend.at[0], grecv.at[t], s, at.twin)
+
+    def x_twin(t, core):
+        return remote(xin.at[2 * t + core], xin.at[2 * t + core], tws.at[0, t], twr.at[0, t], s, at.twin)
+
+    def g_twin(t, core):
+        return remote(gin.at[2 * t + core], gin.at[2 * t + core], tws.at[1, t], twr.at[1, t], s, at.twin)
+
+    for i in range(3):
+        x_send(i).start()
+
+        @pl.when(segs[i] < 2)
+        def _():
+            g_send(i).start()
+
+    def twin_mix(p):
+        mine = pl.ds(pl.multiple_of(2 * STRIP * p + STRIP * (1 - c), STRIP), STRIP)
+        return remote(mix.at[:, mine, :], mrx.at[:, p], msend.at[p], mrecv.at[p], s, at.twin)
+
+    for p in range(4):
+        twin_mix(p).start()
+    xin[2 * s + c] = u[2 * lay]
+    x_twin(s, c).start()
+
+    @pl.when(s < 2)
+    def _():
+        gin[2 * s + c] = g[2]
+        g_twin(s, c).start()
+
+    @pl.when(s >= 2)
+    def _():
+        for t in range(4):
+            seeds[t].wait()
+            g_twin(t, c).start()
+
+    partners = [(s, at.twin), (at.xn, d), (at.yn, d), (s, d + 2 * (1 - 2 * lax.rem(z, 2))), (s, lax.rem(d + 4, 8))]
+
+    def sg_round(r):
+        return remote(sga.at[r], sgr.at[r], sgs.at[r], sgv.at[r], *partners[r])
+
+    sga[0] = sg[...]
+    sg_round(0).start()
+
+    for p in range(4):
+        strips[p].wait()
+        twin_mix(p).wait_recv()
+
+        @pl.loop(0, 8)
+        def _(b):
+            add_into(mown.at[b, p], mrx.at[b, p])
+
+    def plane_send(i, layer):
+        return remote(mown.at[4 * layer + segs[i]], prx.at[i, layer], psend.at[i, layer], precv.at[i, layer], segs[i], d)
+
+    for layer in (1, 0):
+        for i in range(3):
+            plane_send(i, layer).start()
+
+    def sg_next(r):
+        sg_round(r).wait_recv()
+        sga[r + 1] = sga[r] + sgr[r]
+        if r < 4:
+            sg_round(r + 1).start()
+
+    sg_next(0)
+
+    def out_send(i, which):
+        src, dst = (u, sec_out) if which == 0 else (g, grad_out)
+        return remote(src.at[segs[i]], dst.at[s], osend.at[which, i], orecv.at[which, i], segs[i], d)
+
+    keep = [pltpu.make_async_copy(u.at[s], sec_out.at[s], lsem.at[9]), pltpu.make_async_copy(g.at[s], grad_out.at[s], lsem.at[10])]
+    for which in range(2):
+        for i in range(3):
+            out_send(i, which).start()
+        keep[which].start()
+    sg_next(1)
+    weights.wait()
+
+    def feed_rows(i):
+        x, _ = norm_parts(xin[i].astype(F32))
+        n = (x * small[lay, 16:17, :] + small[lay, 17:18, :]).astype(BF16)
+        nbuf[i] = n
+        h = mm(n, fwv[0]) + small[lay, pl.ds(18 + quarter, 1), :]
+        cdf = 0.5 + 0.5 * lax.erf(h * ROOT_HALF)
+        abuf[i] = (h * cdf).astype(BF16)
+        slope = cdf + h * (ROOT_TWO_PI * jnp.exp(-0.5 * h * h))
+        dhbuf[i] = (mm_nt(gin[i], fwv[1]) * slope).astype(BF16)
+
+    for i in range(4):
+        t = s if i == 0 else segs[i - 1]
+        if i > 0:
+            x_arrival(t).wait_recv()
+            x_twin(t, c).start()
+
+            @pl.when(s < 2)
+            def _():
+                g_arrival(t).wait_recv()
+                g_twin(t, c).start()
+
+        if i > 0:
+            sg_next(i + 1)
+        x_twin(t, 1 - c).wait_recv()
+        g_twin(t, 1 - c).wait_recv()
+
+        @pl.loop(0, 2)
+        def _(core):
+            feed_rows(2 * t + core)
+
+    goals = goal_order(z)
+    mix_sum = PlaneSum(at, below_m, above_m, zms, zmb, zma)
+    for layer in (1, 0):
+        for i in range(3):
+            plane_send(i, layer).wait_recv()
+
+            @pl.loop(0, 4)
+            def _(p):
+                add_into(mown.at[4 * layer + s, p], prx.at[i, layer, p])
+
+        for goal in goals[:2]:
+            mix_sum.step(4 * layer + goal, mown.at[4 * layer + s, goal], goal)
+
+    feed_sum = PlaneSum(at, below_f, above_f, zfs, zfb, zfa)
+    stack = lambda ref: ref[...].reshape(8 * ROWS, W)
+
+    def product(out, left, right):
+        for i in range(3):
+            cols = slice(256 * i, 256 * i + 256)
+            lhs = left[:, :, cols].reshape(8 * ROWS, 256)
+            out[cols, :] = mm_tn(lhs, stack(right)).astype(BF16)
+
+    def part(ref, i):
+        return ref.at[pl.ds(pl.multiple_of(2 * STRIP * i, 2 * STRIP), 2 * STRIP), :]
+
+    product(dwe, nbuf, dhbuf)
+    for goal in goals[:2]:
+        feed_sum.step(goal, part(dwe, goal), goal)
+    product(dwr, abuf, gin)
+    for i in range(4):
+        feed_sum.step(4 + i, part(dwr, i), quarter)
+    for goal in goals[2:]:
+        for layer in (1, 0):
+            mix_sum.step(4 * layer + goal, mown.at[4 * layer + s, goal], goal)
+    for goal in goals[2:]:
+        feed_sum.step(goal, part(dwe, goal), goal)
+
+    def unit(kind, layer, j):
+        if kind == "mix":
+            return 4 * layer + j, j, c, fin.at[layer, j], lambda p: mown.at[4 * layer + s, z]
+        if kind == "exp":
+            src = lambda p: dwe.at[pl.ds(pl.multiple_of(2 * STRIP * z + STRIP * p, STRIP), STRIP), :]
+            return 8 + 4 * layer + j, 2 * layer + j // 2, j % 2, fin.at[layer, 4 + j], src
+        src = lambda p: dwr.at[pl.ds(pl.multiple_of(4 * STRIP * p + 2 * STRIP * j, 2 * STRIP), 2 * STRIP), :]
+        return 16 + 2 * layer + j, 2 * layer + z // 2, lax.rem(z, 2), fin.at[layer, pl.ds(8 + 2 * j, 2)], src
+
+    def pieces(kind, layer, j):
+        index, owner, core, dst, src = unit(kind, layer, j)
+        by_x = index % 2 == 0
+        cores = (c,) if kind == "mix" else (0, 1)
+        owns = (s == owner) if kind == "mix" else ((s == owner) & (c == core))
+        sends = []
+        for n, p in enumerate(cores):
+            dev = d if kind == "mix" else 2 * z + p
+            ref = src(p)
+            if kind == "red":
+                ref = [ref.at[pl.ds(0, STRIP), :], ref.at[pl.ds(STRIP, STRIP), :]]
+                targets = [dst.at[0], dst.at[1]]
+            else:
+                ref, targets = [ref], [dst]
+            for m in range(len(ref)):
+                for k, seg in enumerate((at.xn, at.yn)):
+                    sends.append((owns, remote(ref[m], targets[m], fsend.at[index, n, m, k], frecv.at[index, m], seg, dev)))
+                if kind == "mix":
+                    sends.append((owns, pltpu.make_async_copy(ref[m], targets[m], frecv.at[index, m])))
+                else:
+                    sends.append((owns & (c == p), pltpu.make_async_copy(ref[m], targets[m], frecv.at[index, m])))
+                    sends.append((owns & (c != p), remote(ref[m], targets[m], fsend.at[index, n, m, 2], frecv.at[index, m], s, at.twin)))
+        return index, owner, owns, by_x, dst, sends
+
+    def parts_of(kind, dst):
+        return [dst.at[0], dst.at[1]] if kind == "red" else [dst]
+
+    done = []
+    for kind, layer, j in UNITS:
+        index, owner, owns, by_x, dst, sends = pieces(kind, layer, j)
+        for cond, copy in sends:
+            @pl.when(cond)
+            def _():
+                copy.start()
+
+        done.append((kind, index, owner, by_x, dst, sends))
+    for kind, index, owner, by_x, dst, sends in done:
+        first, then = (at.xn, at.yn) if by_x else (at.yn, at.xn)
+        for m, ref in enumerate(parts_of(kind, dst)):
+            relay = remote(ref, ref, fsend.at[index, 0, m, 3], frecv.at[index, m], then, d)
+            relay.wait_recv()
+
+            @pl.when(owner == first)
+            def _():
+                relay.start()
+
+    sg_out[...] = sga[5]
+    for r in range(5):
+        sg_round(r).wait_send()
+    for kind, index, owner, by_x, dst, sends in done:
+        first, then = (at.xn, at.yn) if by_x else (at.yn, at.xn)
+        for cond, copy in sends:
+            if hasattr(copy, "wait_send") and copy.is_remote:
+                @pl.when(cond)
+                def _():
+                    copy.wait_send()
+
+        for m, ref in enumerate(parts_of(kind, dst)):
+            relay = remote(ref, ref, fsend.at[index, 0, m, 3], frecv.at[index, m], then, d)
+
+            @pl.when(owner == first)
+            def _():
+                relay.wait_send()
+
+    for i in range(3):
+        x_send(i).wait_send()
+
+        @pl.when(segs[i] < 2)
+        def _():
+            g_send(i).wait_send()
+
+        for which in range(2):
+            out_send(i, which).wait()
+        for layer in range(2):
+            plane_send(i, layer).wait_send()
+    for t in range(4):
+        x_twin(t, c).wait_send()
+        g_twin(t, c).wait_send()
+    for copy in keep:
+        copy.wait()
+    for p in range(4):
+        twin_mix(p).wait_send()
+    for goal in range(4):
+        for layer in range(2):
+            mix_sum.drain(4 * layer + goal, mown.at[4 * layer + s, goal], goal)
+        feed_sum.drain(goal, part(dwe, goal), goal)
+        feed_sum.drain(4 + goal, part(dwr, goal), quarter)
+
+
+def sum_call(u, g, cot, mix, fw, small, sg):
+    V = pltpu.VMEM
+    D = pltpu.SemaphoreType.DMA
+    S = jax.ShapeDtypeStruct
+    anywhere = pl.BlockSpec(memory_space=pl.ANY)
+    vmem = pl.BlockSpec(memory_space=V)
+    rows = V((8, ROWS, W), BF16)
+    block = V((W, W), BF16)
+    return pl.pallas_call(
+        sum_kernel,
+        out_shape=(S((4, ROWS, W), BF16), S((4, ROWS, W), BF16), S((2, 12, STRIP, W), BF16), S((2, 24, W), F32)),
+        in_specs=[vmem, vmem, anywhere, anywhere, anywhere, vmem, vmem],
+        out_specs=[anywhere, anywhere, anywhere, vmem],
+        scratch_shapes=[
+            rows, rows, rows, rows, rows, V((2, W, W), BF16), block, block,
+            V((8, 4, STRIP, W), BF16), V((8, 4, STRIP, W), BF16), V((3, 2, 4, STRIP, W), BF16),
+            V((8, STRIP, W), BF16), V((8, STRIP, W), BF16), V((8, 2 * STRIP, W), BF16), V((8, 2 * STRIP, W), BF16),
+            V((5, 2, 24, W), F32), V((6, 2, 24, W), F32),
+            D((11,)), D((3,)), D((4,)), D((3,)), D((4,)), D((2, 4)), D((2, 4)), D((2, 3)), D((2, 3)), D((4,)), D((4,)), D((3, 2)), D((3, 2)),
+            D((8,)), D((8,)), D((8,)), D((8,)), D((8,)), D((8,)), D((20, 2, 2, 4)), D((20, 2)), D((5,)), D((5,)),
+        ],
+        compiler_params=pltpu.CompilerParams(collective_id=2, has_side_effects=True, vmem_limit_bytes=60 * 1024 * 1024),
+        name="sum_gradients",
+    )(u, g, cot, mix, fw, small, sg)
 
 
 def pack_small(conv_weight, conv_bias, mixer_gain, mixer_shift, triple_bias, output_bias, feed_gain, feed_shift, expand_bias, reduce_bias):
@@ -1095,43 +1493,20 @@
     own = patches.shape[0] // lax.axis_size("segment")
     mine = lambda v: lax.dynamic_slice_in_dim(v, s * own, own, 0)
     x = pad_images(mine(patches))
-    gin = pad_images(mine(cotangent))
+    cot = pad_images(cotangent).reshape(4, ROWS, W)
+    gin = lax.dynamic_index_in_dim(cot, s, 0, keepdims=False)
     mask = pad_images(mine(region_mask).astype(BF16)[:, None])
-    u, g, sg, w = chain_call(triple_weight, output_weight, expand_weight, reduce_weight, small, x, mask, gin)
-    sections = lambda v: lax.all_to_all(unpad_images(v), "segment", split_axis=0, concat_axis=1, tiled=True)
-    blocks = []
-    for layer in range(2):
-        e_w, r_w = w[12 * layer + 4:12 * layer + 8], w[12 * layer + 8:12 * layer + 12]
-        ui = u[2 * layer].astype(F32)
-        go = g[2] if layer == 0 else gin
-        hat, _ = norm_parts(ui)
-        n = (hat * small[layer, 16] + small[layer, 17]).astype(BF16)
-        es, rs = [], []
-        for j in range(4):
-            h = mm(n, e_w[j]) + small[layer, 18 + j]
-            a, pull = jax.vjp(gelu_exact, h)
-            dh = pull(mm_nt(go, r_w[j]))[0].astype(BF16)
-            es.append(mm_tn(n, dh).astype(BF16))
-            rs.append(mm_tn(a.astype(BF16), go).astype(BF16))
-        blocks.append((w[12 * layer:12 * layer + 4], jnp.stack(es), jnp.stack(rs)))
-    dp = lax.axis_size("dp")
-    by_row = lambda v: v.reshape(4, dp, W // dp, W).transpose(1, 2, 0, 3)
-    total = jnp.concatenate(
-        [jnp.concatenate([by_row(m).reshape(dp, -1, W), by_row(e).reshape(dp, -1, W), r.reshape(dp, -1, W)], axis=1) for m, e, r in blocks], axis=1
-    )
-    total = lax.psum_scatter(total, "dp", scatter_dimension=0, tiled=True)[0]
-    total = lax.psum(total, "segment").astype(F32)
-    part = W // dp
-    total = total.reshape(2, 3, part * 4, W)
-    mix = total[:, 0].reshape(2, part, 4 * W)
-    exp = total[:, 1].reshape(2, part, 4 * W)
-    red = total[:, 2]
-    sg = lax.psum(sg, ("segment", "dp"))
+    u, g, sg, mix, fw = chain_call(triple_weight, output_weight, expand_weight, reduce_weight, small, x, mask, gin)
+    sec_out, grad_out, fin, sg = sum_call(u, g, cot, mix, fw, small, sg)
+    place = lambda v: unpad_images(v.reshape(1, 4 * ROWS, W))
+    part = W // lax.axis_size("dp")
+    fin = fin.astype(F32)
+    wide = lambda lo, hi: jnp.concatenate([fin[:, j] for j in range(lo, hi)], axis=2)
     cut = lambda lo, hi: lax.dynamic_slice_in_dim(sg[:, lo:hi].reshape(2, -1), d * part * (hi - lo), part * (hi - lo), 1)
     taps = lax.dynamic_slice_in_dim(sg[:, :9], d * part, part, 2)
     return (
-        sections(u), sections(g), taps, cut(9, 10), cut(10, 11), cut(11, 12), mix[:, :, :3 * W], cut(12, 15), mix[:, :, 3 * W:],
-        cut(15, 16), cut(16, 17), cut(17, 18), exp, cut(18, 22), red, cut(22, 23),
+        place(sec_out), place(grad_out), taps, cut(9, 10), cut(10, 11), cut(11, 12), wide(0, 3), cut(12, 15), fin[:, 3],
+        cut(15, 16), cut(16, 17), cut(17, 18), wide(4, 8), cut(18, 22), fin[:, 8:].reshape(2, 4 * part, W), cut(22, 23),
     )
 
 

time: 817 us -> 498 us (0.61)
  waiting for transfers between devices: 414 us -> 0 us
  Pallas kernels: 173 us -> 456 us
  local copies, waits for them, and re-layouts: 105 us -> 17 us
  matrix products: 75.4 us -> 0 us
  between operations: 16.3 us -> 1.46 us
    pallas_call x0 -> x1, Pallas kernels: none -> 289 us  [sum_call(): pl.pallas_call(sum_kernel, out_shape=(S((4, ROWS, W), BF16), S((4, ROWS,...]
    reduce_scatter x1 -> x0, waiting for transfers between devices: 281 us -> none  [spread_body(): total = lax.psum_scatter(total, 'dp', scatter_dimension=0, tiled=True)[0]]
    psum x2 -> x0, waiting for transfers between devices: 112 us -> none  [the longest x1 71.1 us: spread_body(): total = lax.psum(total, 'segment').astype(F32)]
    dot_general x24 -> x0, matrix products: 75.4 us -> none  [the longest x16 61.1 us: mm_tn(): lax.dot_general(a, b, (((0,), (0,)), ((), ())), preferred_element_type=F32)]
    concatenate x2 -> x0, local copies, waits for them, and re-layouts: 24.3 us -> none  [spread_body(): jnp.concatenate([jnp.concatenate([by_row(m).reshape(dp, -1, W), by_row(e)...]
    unnamed x63 -> x42, local copies, waits for them, and re-layouts: 23.5 us -> 2.69 us
    all_to_all x2 -> x0, waiting for transfers between devices: 20.6 us -> none  [spread_body(): lax.all_to_all(unpad_images(v), 'segment', split_axis=0, concat_axis=1, t...]
    slice x5 -> x1, local copies, waits for them, and re-layouts: 14.4 us -> 1.61 us  [spread_body(): fin[:, 8:].reshape(2, 4 * part, W)]
  transfers between devices with their start and end apart: 5 -> 0, of which waited for: 4 -> 0; matrix products, arithmetic and copies ran while one was open for 2% -> 0% of each run, Pallas kernels for 0% -> 0%
where the time goes in v2:
time: 498 us; the launch traced here: 494 us
  Pallas kernels  456 us (92%)
  local copies, waits for them, and re-layouts  17 us (3%)
  blocking collectives  12.1 us (2%)
  other arithmetic  7.27 us (1%)
    pallas_call x1, Pallas kernels, sum_call(): pl.pallas_call(sum_kernel, out_shape=(S((4, ROWS, W), BF16), S((4, ROWS,...  289 us
    pallas_call x1, Pallas kernels, chain_call(): pl.pallas_call(chain_kernel, out_shape=(S((4, ROWS, W), BF16), S((4, ROWS...  167 us
    all_gather x1, blocking collectives, spread_body(): small = spread_small(lax.all_gather(packed, 'dp', axis=0)).astype(F32)  12.1 us

profile of v2, /device:TPU:16, one launch (start us, length us, event | category | flops | bytes accessed | tf_op | source)
XLA Modules:
  0.0 494.1 jit_solution(8902338994512877697)
XLA Ops:
  0.8 1.1 constant_dynamic-slice_fusion.10
  2.0 0.8 pad.12
  2.8 0.8 dynamic-slice_convert_fusion
  3.6 0.8 reshape.140.mask
  4.8 12.1 %all-gather = bf16[16,23,96]{2,1,0:T(8,128)(2,1)S(1)} all-gather(bf16[2,23,96]{2,1,0:T(8,128)(2,1)S(1)} %concatenate.12), channel_id=2, replica_groups=mesh['segment'=4,'dp'=8] {'dp'}, dimensions={0}, use_global_device_ids=true | all-gather | bytes 79488 | tf_op jit(solution)/shard_map/all_gather | solution.py:1492
  17.0 0.1 reshape.126
  17.1 0.1 reshape.125
  17.2 0.1 reshape.124
  17.6 0.2 concatenate.13
  17.8 0.7 convert_element_type.15.small
  18.5 0.4 reshape.132
  18.9 0.1 pad.14
  19.1 1.1 copy-done.1
  20.1 0.8 dynamic-slice_bitcast_fusion.gin
  20.9 167.2 %gather_and_chain.1 = (bf16[4,224,768]{2,1,0:T(8,128)(2,1)}, bf16[4,224,768]{2,1,0:T(8,128)(2,1)}, f32[2,24,768]{2,1,0:T(8,128)}, bf16[8,768,768]{2,1,0:T(8,128)(2,1)}, bf16[2,768,768]{2,1,0:T(8,128)(2,1)}) custom-call(bf16[2,96,2304]{2,1,0:T(8,128)(2,1)} %triple.1, bf16[2,96,768]{2,1,0:T(8,128)(2,1)} %output.1, bf16[2,96,3072]{2,1,0:T(8,128)(2,1)} %expand.1, ...), custom_call_target="tpu_custom_call" | custom-call | tf_op jit(solution)/shard_map/gather_and_chain/pallas_call | solution.py:1049
  188.1 289.0 %sum_gradients.1 = (bf16[4,224,768]{2,1,0:T(8,128)(2,1)}, bf16[4,224,768]{2,1,0:T(8,128)(2,1)}, bf16[2,12,96,768]{3,2,1,0:T(8,128)(2,1)}, f32[2,24,768]{2,1,0:T(8,128)}) custom-call(bf16[4,224,768]{2,1,0:T(8,128)(2,1)} %get-tuple-element.25.u, bf16[4,224,768]{2,1,0:T(8,128)(2,1)} %get-tuple-element.26.g, bf16[4,224,768]{2,1,0:T(8,128)(2,1)} %bitcast.85, ...), custom_call_target="tpu_custom_call" | custom-call | tf_op jit(solution)/shard_map/sum_gradients/pallas_call | solution.py:1436
  477.1 2.8 convert_element_type.17
  480.0 1.1 slice_bitcast_fusion.3
  481.1 1.7 pad_maximum_fusion
  482.8 0.6 constant_dynamic-slice_fusion
  483.5 0.6 constant_dynamic-slice_fusion.3
  484.1 1.3 pad_maximum_fusion.1
  485.4 0.6 constant_dynamic-slice_fusion.6
  486.1 0.7 copy-done
  486.7 1.6 slice.119
  488.4 0.2 copy-done.3
  488.6 1.2 reshape.133
  489.8 1.2 reshape.134
  491.1 0.6 copy.101
  491.7 0.6 constant_dynamic-slice_fusion.1
  492.4 0.7 constant_dynamic-slice_fusion.5
  493.0 0.6 constant_dynamic-slice_fusion.8
  (63 shorter events, 1.0 us)
Async XLA Ops:
  0.7 3.8 copy-start.6
  0.7 3.8 copy-start.7
  0.7 3.8 copy-start.8
  0.7 3.9 copy-start.9
  0.7 3.9 copy-start.10
  0.7 3.9 copy-start.11
  0.7 3.9 copy-start.12
  0.7 3.9 copy-start.13
  0.7 4.0 copy-start.14
  0.7 4.0 copy-start.15
  0.8 17.8 %copy-start.4 = (bf16[784,768]{1,0:T(8,128)(2,1)S(1)}, bf16[784,768]{1,0:T(8,128)(2,1)}, u32[]{:S(2)}) copy-start(bf16[784,768]{1,0:T(8,128)(2,1)} %param.33) | copy-start | bytes 3612676
  19.0 1.1 copy-start.1
  481.1 1.7 copy-start.5
  484.1 2.6 copy-start
  486.7 1.8 copy-start.3
  488.4 1.4 copy-start.2
